TPU v7x, 32 devices: a whole 2x2x4 slice. The times are simulated.
32 devices in a mesh: tm: 32 (over z, y, x, core).
Axes of the slice: x: 2, y: 2, z: 4, core: 2. Of those that a mesh axis runs over, the one named last changes fastest.
Arguments:
- measurements: float32 [32, 128], P('tm'), may hold values from -6 to 6
- noise_levels: float32 [32, 128], P('tm'), may hold values from 0.05 to 2
- transition: float32 [256, 256], replicated, may hold values from -0.5 to 1.5
- sensing: float32 [128, 256], replicated, may hold values from -0.75 to 0.75
- process_noise: float32 [256, 256], replicated, may hold values from -0.2 to 0.6, as said below
- prior_mean: float32 [256], replicated, may hold values from -5 to 5
- prior_covariance: float32 [256, 256], replicated, may hold values from -0.6 to 2.5, as said below
Outputs:
- smoothed_means: float32 [32, 256], P('tm')
- smoothed_covariances: float32 [32, 256, 256], P('tm')
Inputs may be any that keep to these rules, and one draw needn't show every extreme that they name: `process_noise`: symmetric positive definite. `prior_covariance`: symmetric positive definite.
All inputs are finite; a program needn't handle non-finite values.
Results may differ from a plain program's by a relative error of at most 0.0003.
Values sent between devices are 32-bit elements; how exact they have to be, the bound alone decides.
No kernel may reach another device: no remote copies, remote signals or barrier semaphores. Data moves between devices by JAX's collectives and lax.ppermute only.
A program may use at most 128 MiB of HBM per device.

v0:
```python
import functools

import jax
import jax.numpy as jnp
from jax import lax
from jax.experimental import pallas as pl
from jax.experimental.pallas import tpu as pltpu
from jax.sharding import PartitionSpec as P

ROWS = 8
LANES = 128
GROUP = 4
BOARD = ROWS * ROWS + ROWS * ROWS // 2
FAN = 4


def dot_nn(left, right):
    return lax.dot_general(
        left,
        right,
        (((1,), (0,)), ((), ())),
        precision=lax.Precision.HIGHEST,
        preferred_element_type=jnp.float32,
    )


def dot_nt(left, right):
    return lax.dot_general(
        left,
        right,
        (((1,), (1,)), ((), ())),
        precision=lax.Precision.HIGHEST,
        preferred_element_type=jnp.float32,
    )


def spread_lane(x, lane):
    return jnp.broadcast_to(x[:, lane : lane + 1], x.shape)


def dot_tn(left, right):
    return lax.dot_general(
        left,
        right,
        (((0,), (0,)), ((), ())),
        precision=lax.Precision.HIGHEST,
        preferred_element_type=jnp.float32,
    )


def factor_small(matrices, board, group):
    side = matrices[0].shape[0]
    count = side // ROWS
    group = min(group, count)
    shape = (ROWS, side)
    row = lax.broadcasted_iota(jnp.int32, shape, 0)
    lane = lax.broadcasted_iota(jnp.int32, shape, 1)
    tasks = [[m[ROWS * k : ROWS * (k + 1)] for k in range(count)] for m in matrices]
    outs = [([], []) for m in matrices]
    for k in range(count):
        base = ROWS * k
        stop = min(count, (k // group + 1) * group)
        for t, (X, out) in enumerate(zip(tasks, outs)):

            def put(slot, values):
                board[t, k % 2, ROWS * slot : ROWS * (slot + 1)] = values

            def spread(slot, r):
                at = ROWS * slot + r
                return jnp.broadcast_to(board[t, k % 2, at : at + 1], shape)

            cols = [spread_lane(X[k], base + i) for i in range(ROWS)]
            for i in range(ROWS):
                put(i, cols[i])
            block = {(r, i): spread(i, r) for i in range(ROWS) for r in range(i, ROWS)}
            nexts = [spread_lane(X[k + 1], base + i) for i in range(ROWS)] if k + 1 < stop else []
            pivots = jnp.ones(shape, jnp.float32)
            for i in range(0, ROWS, 2):
                p = base + i
                pair = (lane == p) | (lane == p + 1)
                a, b, c = block[i, i], block[i + 1, i], block[i + 1, i + 1]
                det = a * c - b * b
                ra = pltpu.reciprocal(a, approx=True)
                rdet = pltpu.reciprocal(det, approx=True)
                ratio = b * ra
                rest = range(i + 2, ROWS)
                firsts = {q: block[q, i] for q in rest}
                mixed = {q: a * block[q, i + 1] - b * firsts[q] for q in rest}
                seconds = {q: mixed[q] * ra for q in rest}
                for q in rest:
                    for r in range(q, ROWS):
                        block[r, q] = (
                            block[r, q] - (firsts[r] * ra) * firsts[q] - (mixed[r] * rdet) * seconds[q]
                        )
                pivots = jnp.where(row == i, a, pivots)
                pivots = jnp.where(row == i + 1, det * ra, pivots)
                put(ROWS + i // 2, X[k])
                xp = spread(ROWS + i // 2, i)
                xp = jnp.where(lane == p, 1.0, jnp.where(lane == p + 1, 0.0, xp))
                xq = spread(ROWS + i // 2, i + 1)
                xq = jnp.where(lane == p + 1, 1.0, jnp.where(lane == p, 0.0, xq))
                xq = xq - ratio * xp
                Z = jnp.where((row == i) & (lane == p), 1.0, X[k])
                if i + 2 < ROWS:
                    f0 = cols[i] * ra
                    f1 = (a * cols[i + 1] - b * cols[i]) * rdet
                    for q in rest:
                        cols[q] = cols[q] - f0 * firsts[q] - f1 * seconds[q]
                    m0 = jnp.where(row > i + 1, f0, 0.0)
                    m1 = jnp.where(row > i + 1, f1, 0.0)
                    Z = jnp.where((row > i + 1) & pair, 0.0, Z) - m0 * xp - m1 * xq
                X[k] = jnp.where(row == i + 1, xq, Z)
                for j in range(k + 1, stop):
                    if j == k + 1:
                        g0, g1 = nexts[i], nexts[i + 1]
                    else:
                        g0 = spread_lane(X[j], p)
                        g1 = spread_lane(X[j], p + 1)
                    h0 = g0 * ra
                    h1 = (a * g1 - b * g0) * rdet
                    if j == k + 1:
                        for q in rest:
                            nexts[q] = nexts[q] - h0 * firsts[q] - h1 * seconds[q]
                    X[j] = jnp.where(pair, 0.0, X[j]) - h0 * xp - h1 * xq
            s = lax.rsqrt(pivots)
            s = s * (1.5 - 0.5 * pivots * s * s)
            scaled = X[k] * s
            diagonal = jnp.where(lane == row + base, pivots * s, 0.0)
            out[0].append(jnp.where(lane > row + base, scaled, diagonal))
            out[1].append(jnp.where(lane <= row + base, scaled, 0.0))
        if k + 1 == stop and stop < count:
            begin = stop - group
            low, high = ROWS * begin, ROWS * stop
            for X, out in zip(tasks, outs):
                uppers = jnp.concatenate(out[0][begin:stop], axis=0)
                lowers = jnp.concatenate(out[1][begin:stop], axis=0)
                after = lax.broadcasted_iota(jnp.int32, uppers.shape, 1) >= high
                change = dot_tn(uppers, jnp.where(after, uppers, lowers))
                here = (lane >= low) & (lane < high)
                for j in range(stop, count):
                    X[j] = jnp.where(here, 0.0, X[j]) - change[ROWS * j : ROWS * (j + 1)]
    return [(jnp.concatenate(u, axis=0), jnp.concatenate(v, axis=0)) for u, v in outs]


def factor(matrices, board):
    blocks = matrices[0].shape[0] // LANES
    if blocks == 1:
        return factor_small(matrices, board, GROUP)

    def cut(m, i, j):
        return m[LANES * i : LANES * (i + 1), LANES * j : LANES * (j + 1)]

    zero = jnp.zeros((LANES, LANES), jnp.float32)
    uppers = [{} for m in matrices]
    lowers = [{} for m in matrices]
    inverses = [{} for m in matrices]
    for j in range(blocks):
        heads = []
        for m, U, L in zip(matrices, uppers, lowers):
            head = cut(m, j, j)
            for k in range(j):
                head = head - dot_nt(L[j, k], L[j, k])
            heads.append(head)
        for m, U, L, V, (u, v) in zip(
            matrices, uppers, lowers, inverses, factor_small(heads, board, GROUP)
        ):
            U[j, j] = u
            V[j, j] = v
            for i in range(j + 1, blocks):
                right = cut(m, j, i)
                down = cut(m, i, j)
                for k in range(j):
                    right = right - dot_nn(L[j, k], U[k, i])
                    down = down - dot_nn(L[i, k], U[k, j])
                U[j, i] = dot_nn(v, right)
                L[i, j] = dot_nt(down, v)
    outs = []
    for U, L, V in zip(uppers, lowers, inverses):
        for i in range(blocks):
            for j in range(i):
                total = dot_nn(L[i, j], V[j, j])
                for k in range(j + 1, i):
                    total = total + dot_nn(L[i, k], V[k, j])
                V[i, j] = -dot_nn(V[i, i], total)
        whole = [
            jnp.concatenate(
                [
                    jnp.concatenate([D.get((i, j), zero) for j in range(blocks)], axis=1)
                    for i in range(blocks)
                ],
                axis=0,
            )
            for D in (U, V)
        ]
        outs.append(tuple(whole))
    return outs


def unit(side):
    row = lax.broadcasted_iota(jnp.int32, (side, side), 0)
    col = lax.broadcasted_iota(jnp.int32, (side, side), 1)
    return jnp.where(row == col, 1.0, 0.0)


def first_of(values):
    row = lax.broadcasted_iota(jnp.int32, (ROWS, values.shape[1]), 0)
    return jnp.where(row == 0, values, 0.0)


def maps_kernel(transition_ref, sensing_ref, noise_ref, maps_ref, consts_ref):
    n = transition_ref.shape[0]
    transition = transition_ref[...]
    sensing = sensing_ref[...]
    noise = noise_ref[...]
    maps_ref[0:n] = transition
    maps_ref[n:] = dot_nn(sensing, transition)
    noise_sensed = dot_nt(noise, sensing)
    consts_ref[0:n, 0:n] = noise
    consts_ref[0:n, n:] = noise_sensed
    consts_ref[n:, 0:n] = jnp.zeros((sensing.shape[0], n), jnp.float32)
    consts_ref[n:, n:] = dot_nn(sensing, noise_sensed)


def window_kernel(
    steps,
    times,
    begin_ref,
    rows_ref,
    maps_ref,
    consts_ref,
    mean_ref,
    prior_ref,
    state_ref,
    info_ref,
    moved_ref,
    waiting_ref,
    inverse_ref,
    sensed_ref,
    board,
):
    n = prior_ref.shape[0]
    o = maps_ref.shape[0] - n
    begin = begin_ref[0]
    eye_sense = unit(o)

    def wrap(t):
        return jnp.where(t >= times, t - times, t)

    def line_at(k):
        return rows_ref[pl.ds(jnp.minimum(k, steps - 1), 1), :]

    def first_spread(k, spread):
        line = line_at(k)
        return spread + consts_ref[n:, n:] + eye_sense * line[:, o:]

    moved_ref[0:n] = jnp.zeros((n, n), jnp.float32)
    moved_ref[n : 2 * n] = unit(n)
    moved_ref[2 * n :] = jnp.zeros((ROWS, n), jnp.float32)
    waiting_ref[...] = jnp.zeros_like(waiting_ref)
    inverse_ref[...] = jnp.zeros_like(inverse_ref)
    info_ref[...] = jnp.zeros_like(info_ref)
    sensed = maps_ref[n:]
    fresh = begin == 0
    sensed_ref[...] = first_spread(
        0, jnp.where(fresh, dot_nn(sensed, dot_nt(prior_ref[...], sensed)), 0.0)
    )

    def update():
        white = dot_nt(waiting_ref[...], inverse_ref[...])
        info_ref[...] = info_ref[...] + dot_nt(white[n:], white[n : 2 * n])
        return moved_ref[...] - dot_nt(white, white[0:n])

    def step(k, carry):
        ((_, inverse),) = factor_small([sensed_ref[...]], board, o // ROWS)
        now = wrap(begin + k)
        later = wrap(now + 1)
        state = update()
        state = jnp.where(
            now == 0,
            jnp.concatenate(
                [prior_ref[...], jnp.zeros((n, n), jnp.float32), first_of(mean_ref[...])], axis=0
            ),
            state,
        )
        moved = dot_nt(state, maps_ref[...])
        ahead = dot_nn(maps_ref[0:n], moved[0:n]) + consts_ref[0:n]
        moved_ref[0:n] = ahead[:, 0:n]
        moved_ref[n:] = moved[n:, 0:n]
        waiting_ref[0:n] = ahead[:, n:]
        waiting_ref[n : 2 * n] = moved[n : 2 * n, n:]
        waiting_ref[2 * n :] = moved[2 * n :, n:] - first_of(line_at(k)[:, 0:o])
        spread = jnp.where(later == 0, prior_ref[...], ahead[:, 0:n])
        kept = dot_nn(maps_ref[n:], dot_nt(spread, maps_ref[n:]))
        gained = dot_nt(dot_nn(maps_ref[n:], ahead[:, n:]), inverse)
        gained = jnp.where(later == 0, 0.0, gained)
        sensed_ref[...] = first_spread(k + 1, kept - dot_nt(gained, gained))
        inverse_ref[...] = inverse
        return carry

    lax.fori_loop(0, steps, step, 0)
    state_ref[...] = update()


def meet_kernel(
    role_ref, state_ref, info_ref, far_state_ref, far_info_ref, mean_ref, cov_ref, board
):
    n = state_ref.shape[1]
    late = role_ref[0] == 1
    eye = unit(n)

    def of_cut(rows, near, far):
        return jnp.where(late, far[rows], near[rows])

    def of_middle(rows, near, far):
        return jnp.where(late, near[rows], far[rows])

    spread_rows, move_rows, center_rows = slice(0, n), slice(n, 2 * n), slice(2 * n, 2 * n + ROWS)
    info_rows, vector_rows = slice(0, n), slice(n, n + ROWS)
    cut_spread = of_cut(spread_rows, state_ref, far_state_ref)
    cut_center = of_cut(center_rows, state_ref, far_state_ref)
    cut_info = of_cut(info_rows, info_ref, far_info_ref)
    cut_vector = of_cut(vector_rows, info_ref, far_info_ref)
    mid_spread = of_middle(spread_rows, state_ref, far_state_ref)
    move = of_middle(move_rows, state_ref, far_state_ref)
    mid_center = of_middle(center_rows, state_ref, far_state_ref)
    mid_info = of_middle(info_rows, info_ref, far_info_ref)
    mid_vector = of_middle(vector_rows, info_ref, far_info_ref)

    (mid_root, _), (cut_root, _) = factor([mid_spread, cut_spread], board)
    rooted = dot_nt(cut_info, mid_root)
    ((_, inner),) = factor([eye + dot_nn(mid_root, rooted)], board)
    carried = dot_nn(inner, mid_root)
    mixing = dot_nt(rooted, inner)
    kept = cut_info - dot_nt(mixing, mixing)
    early_info = mid_info + dot_nt(dot_nn(move, kept), move)
    ((_, last),) = factor(
        [eye + dot_nn(cut_root, dot_nt(early_info, cut_root))], board
    )
    residue = -cut_vector - dot_nn(mid_center, cut_info)
    residue_carried = dot_nt(residue, carried)
    early_vector = dot_nt(residue - dot_nt(residue_carried, mixing), move) - mid_vector
    pull = early_vector - dot_nn(cut_center, early_info)
    cut_root_t = cut_root.T
    through = move - dot_nn(dot_nn(move, mixing), carried)
    through_center = mid_center + dot_nn(residue_carried, carried)
    carried_t = carried.T
    leftover = dot_nt(carried_t, carried_t)
    late_root = dot_nt(through.T, cut_root)
    early_root = dot_nt(cut_root_t, last)
    early_center = cut_center + dot_nt(dot_nn(pull, early_root), early_root)
    root = dot_nt(jnp.where(late, late_root, cut_root_t), last)
    cov_ref[0] = jnp.where(late, leftover, 0.0) + dot_nt(root, root)
    late_center = dot_nn(early_center, through) + through_center
    mean_ref[...] = jnp.where(late, late_center, early_center)[0:1]


def begin_of(device, devices):
    quarter = devices // 4
    chip = device // 2
    upper = chip // quarter
    split = 2 * (chip - quarter * upper) + upper
    role = device % 2
    return (split + 1 + (1 - role) * (devices - devices // 2)) % devices


def gather_rows(rows, steps, axis):
    devices = lax.axis_size(axis)
    begins = [begin_of(i, devices) for i in range(devices)]
    holder = {begin: i for i, begin in enumerate(begins)}
    held = min(FAN, steps)
    parts = [
        lax.ppermute(rows, axis, [((begins[i] + j) % devices, i) for i in range(devices)])
        for j in range(held)
    ]
    rows = jnp.concatenate(parts, axis=0)
    while held < steps:
        parts = [rows]
        for m in range(1, FAN):
            size = min(held, steps - m * held)
            if size > 0:
                pairs = [(holder[(begins[i] + m * held) % devices], i) for i in range(devices)]
                parts.append(lax.ppermute(rows[:size], axis, pairs))
        rows = jnp.concatenate(parts, axis=0)
        held = min(steps, FAN * held)
    return rows


def shards(
    measurements, noise_levels, transition, sensing, process_noise, prior_mean, prior_covariance
):
    n = transition.shape[0]
    o = sensing.shape[0]
    devices = lax.axis_size("tm")
    half = devices // 2
    device = lax.axis_index("tm").astype(jnp.int32)
    role = device % 2
    begin = begin_of(device, devices)

    rows = gather_rows(jnp.concatenate([measurements, noise_levels], axis=1), half, "tm")
    vmem = pl.BlockSpec(memory_space=pltpu.VMEM)
    smem = pl.BlockSpec(memory_space=pltpu.SMEM)
    params = pltpu.CompilerParams(vmem_limit_bytes=48 * 1024 * 1024)

    def shape(*dims):
        return jax.ShapeDtypeStruct(dims, jnp.float32)

    maps, consts = pl.pallas_call(
        maps_kernel,
        out_shape=(shape(n + o, n), shape(n + o, n + o)),
        in_specs=[vmem] * 3,
        out_specs=(vmem, vmem),
        compiler_params=params,
    )(transition, sensing, process_noise)
    state, info = pl.pallas_call(
        functools.partial(window_kernel, half, devices),
        out_shape=(shape(2 * n + ROWS, n), shape(n + ROWS, n)),
        in_specs=[smem] + [vmem] * 5,
        out_specs=(vmem, vmem),
        scratch_shapes=[
            pltpu.VMEM((2 * n + ROWS, n), jnp.float32),
            pltpu.VMEM((2 * n + ROWS, o), jnp.float32),
            pltpu.VMEM((o, o), jnp.float32),
            pltpu.VMEM((o, o), jnp.float32),
            pltpu.VMEM((1, 2, BOARD, o), jnp.float32),
        ],
        compiler_params=params,
    )(begin.reshape(1), rows, maps, consts, prior_mean.reshape(1, n), prior_covariance)
    swap = [(i, i ^ 1) for i in range(devices)]
    far_state = lax.ppermute(state, "tm", swap)
    far_info = lax.ppermute(info, "tm", swap)
    mean, cov = pl.pallas_call(
        meet_kernel,
        out_shape=(shape(1, n), shape(1, n, n)),
        in_specs=[smem] + [vmem] * 4,
        out_specs=(vmem, vmem),
        scratch_shapes=[pltpu.VMEM((2, 2, BOARD, LANES), jnp.float32)],
        compiler_params=params,
    )(role.reshape(1), state, info, far_state, far_info)
    home = []
    for i in range(devices):
        above = i >= half
        spot = 2 * ((i - half if above else i) // 2) + (1 if above else 0)
        home.append((i, spot + half if i % 2 else spot))
    return lax.ppermute(mean, "tm", home), lax.ppermute(cov, "tm", home)


def solution(mesh):
    return jax.shard_map(
        shards,
        mesh=mesh,
        in_specs=(P("tm", None), P("tm", None), P(), P(), P(), P(), P()),
        out_specs=(P("tm", None), P("tm", None, None)),
        check_vma=False,
    )
```

profile of v0, /device:TPU:1, one launch (start us, length us, event | category | flops | bytes accessed | tf_op | source)
XLA Modules:
  0.0 168.5 jit_solution(4062709226746261429)
XLA Ops:
  0.6 0.0 copy-start.5
  0.6 0.7 constant_dynamic-update-slice_fusion.1
  1.3 0.0 copy-done.5
  1.3 5.7 %collective-permute-start.3 = (f32[1,256]{1,0:T(1,128)S(1)}, f32[1,256]{1,0:T(1,128)S(1)}, u32[]{:S(2)}, u32[]{:S(2)}) collective-permute-start(f32[1,256]{1,0:T(1,128)S(1)} %constant_dynamic-update-slice_fusion), channel_id=1, source_target_pairs={{20,0},{4,1},{22,2},{6,3},{24,4},{8,5},{26,6},{10,7},{28,8},{12,9}... | collective-permute-start | bytes 3080 | tf_op jit(solution)/shard_map/ppermute | solution.py:372
  7.0 0.0 collective-permute-start.2
  7.0 2.6 %collective-permute-start.1 = (f32[1,256]{1,0:T(1,128)S(1)}, f32[1,256]{1,0:T(1,128)S(1)}, u32[]{:S(2)}, u32[]{:S(2)}) collective-permute-start(f32[1,256]{1,0:T(1,128)S(1)} %constant_dynamic-update-slice_fusion), channel_id=1, source_target_pairs={{18,0},{2,1},{20,2},{4,3},{22,4},{6,5},{24,6},{8,7},{26,8},{10,9},... | collective-permute-start | bytes 3080 | tf_op jit(solution)/shard_map/ppermute | solution.py:372
  9.6 0.6 collective-permute-start
  10.3 0.0 collective-permute-done.3
  10.3 0.0 collective-permute-done.2
  10.3 0.0 collective-permute-done.1
  10.3 0.0 collective-permute-done
  10.3 5.4 %collective-permute-start.6 = (f32[4,256]{1,0:T(4,128)S(1)}, f32[4,256]{1,0:T(4,128)S(1)}, u32[]{:S(2)}, u32[]{:S(2)}) collective-permute-start(f32[4,256]{1,0:T(4,128)S(1)} %pad_maximum_fusion), channel_id=1, source_target_pairs={{12,0},{13,1},{14,2},{15,3},{1,4},{0,5},{3,6},{2,7},{5,8},{4,9},{7... | collective-permute-start | bytes 12296 | tf_op jit(solution)/shard_map/ppermute | solution.py:382
  15.8 0.0 collective-permute-start.5
  15.8 2.6 %collective-permute-start.4 = (f32[4,256]{1,0:T(4,128)S(1)}, f32[4,256]{1,0:T(4,128)S(1)}, u32[]{:S(2)}, u32[]{:S(2)}) collective-permute-start(f32[4,256]{1,0:T(4,128)S(1)} %pad_maximum_fusion), channel_id=1, source_target_pairs={{4,0},{5,1},{6,2},{7,3},{8,4},{9,5},{10,6},{11,7},{12,8},{13,9},{1... | collective-permute-start | bytes 12296 | tf_op jit(solution)/shard_map/ppermute | solution.py:382
  18.3 0.0 copy-start
  18.3 0.9 copy-done
  19.3 0.0 copy-start.1
  19.3 0.9 copy-done.1
  20.2 0.0 copy-start.3
  20.2 0.9 copy-done.3
  21.1 0.0 copy-start.2
  21.1 0.9 shard_map.86
  22.0 0.0 collective-permute-done.6
  22.1 0.0 collective-permute-done.5
  22.1 0.0 collective-permute-done.4
  22.1 0.0 copy-start.4
  22.1 0.0 copy-done.2
  22.1 0.7 copy-done.4
  22.8 93.2 %shard_map.87 = (f32[520,256]{1,0:T(8,128)S(1)}, f32[264,256]{1,0:T(8,128)S(1)}) custom-call(s32[1]{0:T(128)} %bitcast.1.begin_ref, f32[16,256]{1,0:T(8,128)S(1)} %concatenate.12.rows_ref, f32[384,256]{1,0:T(8,128)S(1)} %get-tuple-element.8.maps_ref, f32[384,384]{1,0:T(8,128)S(1)} %get-tuple-element.9.consts_ref, f32[1,256]{1,0:T(1,128)S(1)} %bitcast.3, ...), custom_call_target="tpu_custom_call" | custom-call | tf_op jit(solution)/shard_map/pallas_call | solution.py:414
  116.0 0.1 collective-permute-start.7
  116.1 0.5 collective-permute-start.8
  116.6 1.8 %collective-permute-done.8.far_info_ref = f32[264,256]{1,0:T(8,128)S(1)} collective-permute-done((f32[264,256]{1,0:T(8,128)S(1)}, f32[264,256]{1,0:T(8,128)S(1)}, u32[]{:S(2)}, u32[]{:S(2)}) %collective-permute-start.8) | collective-permute-done | bytes 270368 | tf_op jit(solution)/shard_map/ppermute | solution.py:430
  118.4 0.0 collective-permute-done.7.far_state_ref
  118.4 37.4 %shard_map.88 = (f32[1,256]{1,0:T(1,128)S(1)}, f32[1,256,256]{2,1,0:T(8,128)S(1)}) custom-call(s32[1]{0:T(128)} %bitcast.role_ref, f32[520,256]{1,0:T(8,128)S(1)} %get-tuple-element.10.state_ref, f32[264,256]{1,0:T(8,128)S(1)} %get-tuple-element.11.info_ref, f32[520,256]{1,0:T(8,128)S(1)} %collective-permute-done.7.far_state_ref, ...), custom_call_target="tpu_custom_call" | custom-call | tf_op jit(solution)/shard_map/pallas_call | solution.py:431
  155.8 4.4 %collective-permute-start.10 = (f32[1,256,256]{2,1,0:T(8,128)S(1)}, f32[1,256,256]{2,1,0:T(8,128)S(1)}, u32[]{:S(2)}, u32[]{:S(2)}) collective-permute-start(f32[1,256,256]{2,1,0:T(8,128)S(1)} %get-tuple-element.13), channel_id=1, source_target_pairs={{0,0},{1,16},{2,2},{3,18},{4,4},{5,20},{6,6},{7,22},{8,8},{9,24},{... | collective-permute-start | bytes 786440 | tf_op jit(solution)/shard_map/ppermute | solution.py:444
  160.2 2.1 %collective-permute-start.9 = (f32[1,256]{1,0:T(1,128)S(1)}, f32[1,256]{1,0:T(1,128)S(1)}, u32[]{:S(2)}, u32[]{:S(2)}) collective-permute-start(f32[1,256]{1,0:T(1,128)S(1)} %get-tuple-element.12), channel_id=1, source_target_pairs={{0,0},{1,16},{2,2},{3,18},{4,4},{5,20},{6,6},{7,22},{8,8},{9,24},{... | collective-permute-start | bytes 3080 | tf_op jit(solution)/shard_map/ppermute | solution.py:444
  162.3 5.0 %collective-permute-done.9 = f32[1,256]{1,0:T(1,128)S(1)} collective-permute-done((f32[1,256]{1,0:T(1,128)S(1)}, f32[1,256]{1,0:T(1,128)S(1)}, u32[]{:S(2)}, u32[]{:S(2)}) %collective-permute-start.9) | collective-permute-done | bytes 1056 | tf_op jit(solution)/shard_map/ppermute | solution.py:444
  167.2 0.0 collective-permute-done.10
  167.3 0.6 copy.12
  167.8 0.7 copy.13
  (3 shorter events, 0.1 us)
Async XLA Ops:
  0.6 0.7 copy-start.5
  1.3 8.9 %collective-permute-start.3 = (f32[1,256]{1,0:T(1,128)S(1)}, f32[1,256]{1,0:T(1,128)S(1)}, u32[]{:S(2)}, u32[]{:S(2)}) collective-permute-start(f32[1,256]{1,0:T(1,128)S(1)} %constant_dynamic-update-slice_fusion), channel_id=1, source_target_pairs={{20,0},{4,1},{22,2},{6,3},{24,4},{8,5},{26,6},{10,7},{28,8},{12,9}... | collective-permute-start | bytes 3080 | tf_op jit(solution)/shard_map/ppermute | solution.py:372
  7.0 3.3 %collective-permute-start.2 = (f32[1,256]{1,0:T(1,128)S(1)}, f32[1,256]{1,0:T(1,128)S(1)}, u32[]{:S(2)}, u32[]{:S(2)}) collective-permute-start(f32[1,256]{1,0:T(1,128)S(1)} %constant_dynamic-update-slice_fusion), channel_id=1, source_target_pairs={{19,0},{3,1},{21,2},{5,3},{23,4},{7,5},{25,6},{9,7},{27,8},{11,9},... | collective-permute-start | bytes 3080 | tf_op jit(solution)/shard_map/ppermute | solution.py:372
  7.0 3.3 %collective-permute-start.1 = (f32[1,256]{1,0:T(1,128)S(1)}, f32[1,256]{1,0:T(1,128)S(1)}, u32[]{:S(2)}, u32[]{:S(2)}) collective-permute-start(f32[1,256]{1,0:T(1,128)S(1)} %constant_dynamic-update-slice_fusion), channel_id=1, source_target_pairs={{18,0},{2,1},{20,2},{4,3},{22,4},{6,5},{24,6},{8,7},{26,8},{10,9},... | collective-permute-start | bytes 3080 | tf_op jit(solution)/shard_map/ppermute | solution.py:372
  9.6 0.7 collective-permute-start
  10.3 11.7 %collective-permute-start.6 = (f32[4,256]{1,0:T(4,128)S(1)}, f32[4,256]{1,0:T(4,128)S(1)}, u32[]{:S(2)}, u32[]{:S(2)}) collective-permute-start(f32[4,256]{1,0:T(4,128)S(1)} %pad_maximum_fusion), channel_id=1, source_target_pairs={{12,0},{13,1},{14,2},{15,3},{1,4},{0,5},{3,6},{2,7},{5,8},{4,9},{7... | collective-permute-start | bytes 12296 | tf_op jit(solution)/shard_map/ppermute | solution.py:382
  15.8 6.3 %collective-permute-start.5 = (f32[4,256]{1,0:T(4,128)S(1)}, f32[4,256]{1,0:T(4,128)S(1)}, u32[]{:S(2)}, u32[]{:S(2)}) collective-permute-start(f32[4,256]{1,0:T(4,128)S(1)} %pad_maximum_fusion), channel_id=1, source_target_pairs={{8,0},{9,1},{10,2},{11,3},{12,4},{13,5},{14,6},{15,7},{1,8},{0,9},... | collective-permute-start | bytes 12296 | tf_op jit(solution)/shard_map/ppermute | solution.py:382
  15.8 6.3 %collective-permute-start.4 = (f32[4,256]{1,0:T(4,128)S(1)}, f32[4,256]{1,0:T(4,128)S(1)}, u32[]{:S(2)}, u32[]{:S(2)}) collective-permute-start(f32[4,256]{1,0:T(4,128)S(1)} %pad_maximum_fusion), channel_id=1, source_target_pairs={{4,0},{5,1},{6,2},{7,3},{8,4},{9,5},{10,6},{11,7},{12,8},{13,9},{1... | collective-permute-start | bytes 12296 | tf_op jit(solution)/shard_map/ppermute | solution.py:382
  18.3 0.9 copy-start
  19.3 0.9 copy-start.1
  20.2 0.9 copy-start.3
  21.1 1.0 copy-start.2
  22.1 0.7 copy-start.4
  116.0 2.4 %collective-permute-start.7 = (f32[520,256]{1,0:T(8,128)S(1)}, f32[520,256]{1,0:T(8,128)S(1)}, u32[]{:S(2)}, u32[]{:S(2)}) collective-permute-start(f32[520,256]{1,0:T(8,128)S(1)} %get-tuple-element.10.state_ref), channel_id=1, source_target_pairs={{0,1},{1,0},{2,3},{3,2},{4,5},{5,4},{6,7},{7,6},{8,9},{9,8},{10,11... | collective-permute-start | bytes 1597448 | tf_op jit(solution)/shard_map/ppermute | solution.py:429
  116.1 2.3 %collective-permute-start.8 = (f32[264,256]{1,0:T(8,128)S(1)}, f32[264,256]{1,0:T(8,128)S(1)}, u32[]{:S(2)}, u32[]{:S(2)}) collective-permute-start(f32[264,256]{1,0:T(8,128)S(1)} %get-tuple-element.11.info_ref), channel_id=1, source_target_pairs={{0,1},{1,0},{2,3},{3,2},{4,5},{5,4},{6,7},{7,6},{8,9},{9,8},{10,11... | collective-permute-start | bytes 811016 | tf_op jit(solution)/shard_map/ppermute | solution.py:430
  155.8 11.5 %collective-permute-start.10 = (f32[1,256,256]{2,1,0:T(8,128)S(1)}, f32[1,256,256]{2,1,0:T(8,128)S(1)}, u32[]{:S(2)}, u32[]{:S(2)}) collective-permute-start(f32[1,256,256]{2,1,0:T(8,128)S(1)} %get-tuple-element.13), channel_id=1, source_target_pairs={{0,0},{1,16},{2,2},{3,18},{4,4},{5,20},{6,6},{7,22},{8,8},{9,24},{... | collective-permute-start | bytes 786440 | tf_op jit(solution)/shard_map/ppermute | solution.py:444
  160.2 7.1 %collective-permute-start.9 = (f32[1,256]{1,0:T(1,128)S(1)}, f32[1,256]{1,0:T(1,128)S(1)}, u32[]{:S(2)}, u32[]{:S(2)}) collective-permute-start(f32[1,256]{1,0:T(1,128)S(1)} %get-tuple-element.12), channel_id=1, source_target_pairs={{0,0},{1,16},{2,2},{3,18},{4,4},{5,20},{6,6},{7,22},{8,8},{9,24},{... | collective-permute-start | bytes 3080 | tf_op jit(solution)/shard_map/ppermute | solution.py:444
where the time goes:
time: 169 us
  Pallas kernels  132 us (78%)
  starting transfers between devices  23.9 us (14%)
  waiting for transfers between devices  6.85 us (4%)
  local copies, waits for them, and re-layouts  5.46 us (3%)
    pallas_call x1, Pallas kernels, shards(): pl.pallas_call(functools.partial(window_kernel, half, devices), out_shape...  93.2 us
    pallas_call x1, Pallas kernels, shards(): pl.pallas_call(meet_kernel, out_shape=(shape(1, n), shape(1, n, n)), in_s...  37.4 us
    ppermute x4, starting transfers between devices, gather_rows(): lax.ppermute(rows, axis, [((begins[i] + j) % devices, i) for i in range(d...  8.93 us
    ppermute x3, starting transfers between devices, gather_rows(): parts.append(lax.ppermute(rows[:size], axis, pairs))  7.98 us
    ppermute x2, starting transfers between devices, shards(): return (lax.ppermute(mean, 'tm', home), lax.ppermute(cov, 'tm', home))  6.46 us
    unnamed x15, local copies, waits for them, and re-layouts  5.41 us
    ppermute x2, waiting for transfers between devices, shards(): return (lax.ppermute(mean, 'tm', home), lax.ppermute(cov, 'tm', home))  4.98 us
  transfers between devices with their start and end apart: 11, of which 2 were waited for; matrix products, arithmetic and copies ran while one was open for 0% of the time, Pallas kernels for 1%

commit v1 on v0

--- a/solution.py
+++ b/solution.py
@@ -10,7 +10,10 @@
 ROWS = 8
 LANES = 128
 GROUP = 4
-BOARD = ROWS * ROWS + ROWS * ROWS // 2
+LEAD = 1
+VECTOR = 16
+EXTRA = ROWS + ROWS // 2
+BOARD = ROWS * (EXTRA + ROWS)
 FAN = 4
 
 
@@ -34,18 +37,84 @@
     )
 
 
+def pieces(x, count):
+    out = []
+    for _ in range(count):
+        out.append(x.astype(jnp.bfloat16))
+        x = x - out[-1].astype(jnp.float32)
+    return out
+
+
+def left_of(x):
+    high, low = pieces(x, 2)
+    return jnp.concatenate([high, low, high], axis=1)
+
+
+def right_of(x):
+    high, low = pieces(x, 2)
+    return jnp.concatenate([high, high, low], axis=1)
+
+
+def left_moving(x):
+    high, low = pieces(x, 2)
+    return jnp.concatenate([high, low, high, high], axis=1)
+
+
+def right_moving(x):
+    high, low = pieces(x, 2)
+    return jnp.concatenate([high, high, high, low], axis=0)
+
+
+def join_nn(left, right):
+    return lax.dot_general(
+        left, right, (((1,), (0,)), ((), ())), preferred_element_type=jnp.float32
+    )
+
+
+def join_nt(left, right):
+    return lax.dot_general(
+        left, right, (((1,), (1,)), ((), ())), preferred_element_type=jnp.float32
+    )
+
+
 def spread_lane(x, lane):
     return jnp.broadcast_to(x[:, lane : lane + 1], x.shape)
 
 
-def dot_tn(left, right):
+def exact_tn(left, right):
+    a, b, c = pieces(left, 3)
+    p, q, r = pieces(right, 3)
     return lax.dot_general(
-        left,
-        right,
+        jnp.concatenate([a, a, b, a, b, c], axis=0),
+        jnp.concatenate([p, q, p, r, q, p], axis=0),
         (((0,), (0,)), ((), ())),
-        precision=lax.Precision.HIGHEST,
         preferred_element_type=jnp.float32,
     )
+
+
+def exact_nt(left, right):
+    a, b, c = pieces(left, 3)
+    p, q, r = pieces(right, 3)
+    return join_nt(
+        jnp.concatenate([a, a, b, a, b, c], axis=1), jnp.concatenate([p, q, p, r, q, p], axis=1)
+    )
+
+
+def exact_nn(left, right):
+    a, b, c = pieces(left, 3)
+    p, q, r = pieces(right, 3)
+    return join_nn(
+        jnp.concatenate([a, a, b, a, b, c], axis=1), jnp.concatenate([p, q, p, r, q, p], axis=0)
+    )
+
+
+def near_nn(left, right):
+    high, low = pieces(right, 2)
+    return join_nn(left_of(left), jnp.concatenate([high, high, low], axis=0))
+
+
+def near_nt(left, right):
+    return join_nt(left_of(left), right_of(right))
 
 
 def factor_small(matrices, board, group):
@@ -57,9 +126,12 @@
     lane = lax.broadcasted_iota(jnp.int32, shape, 1)
     tasks = [[m[ROWS * k : ROWS * (k + 1)] for k in range(count)] for m in matrices]
     outs = [([], []) for m in matrices]
+    heads = [[spread_lane(X[0], i) for i in range(ROWS)] for X in tasks]
     for k in range(count):
         base = ROWS * k
+        more = k + 1 < count
         stop = min(count, (k // group + 1) * group)
+        reach = min(count, stop + LEAD)
         for t, (X, out) in enumerate(zip(tasks, outs)):
 
             def put(slot, values):
@@ -69,11 +141,12 @@
                 at = ROWS * slot + r
                 return jnp.broadcast_to(board[t, k % 2, at : at + 1], shape)
 
-            cols = [spread_lane(X[k], base + i) for i in range(ROWS)]
+            cols = heads[t]
             for i in range(ROWS):
                 put(i, cols[i])
             block = {(r, i): spread(i, r) for i in range(ROWS) for r in range(i, ROWS)}
-            nexts = [spread_lane(X[k + 1], base + i) for i in range(ROWS)] if k + 1 < stop else []
+            nexts = [spread_lane(X[k + 1], base + i) for i in range(ROWS)] if more else []
+            heads[t] = [spread_lane(X[k + 1], base + ROWS + i) for i in range(ROWS)] if more else []
             pivots = jnp.ones(shape, jnp.float32)
             for i in range(0, ROWS, 2):
                 p = base + i
@@ -110,15 +183,21 @@
                     m1 = jnp.where(row > i + 1, f1, 0.0)
                     Z = jnp.where((row > i + 1) & pair, 0.0, Z) - m0 * xp - m1 * xq
                 X[k] = jnp.where(row == i + 1, xq, Z)
-                for j in range(k + 1, stop):
+                for j in range(k + 1, reach):
                     if j == k + 1:
                         g0, g1 = nexts[i], nexts[i + 1]
                     else:
                         g0 = spread_lane(X[j], p)
                         g1 = spread_lane(X[j], p + 1)
                     h0 = g0 * ra
-                    h1 = (a * g1 - b * g0) * rdet
+                    g1 = a * g1 - b * g0
+                    h1 = g1 * rdet
                     if j == k + 1:
+                        put(EXTRA + i, g0)
+                        put(EXTRA + i + 1, g1 * ra)
+                        for q in range(ROWS):
+                            first, second = spread(EXTRA + i, q), spread(EXTRA + i + 1, q)
+                            heads[t][q] = heads[t][q] - h0 * first - h1 * second
                         for q in rest:
                             nexts[q] = nexts[q] - h0 * firsts[q] - h1 * seconds[q]
                     X[j] = jnp.where(pair, 0.0, X[j]) - h0 * xp - h1 * xq
@@ -128,16 +207,16 @@
             diagonal = jnp.where(lane == row + base, pivots * s, 0.0)
             out[0].append(jnp.where(lane > row + base, scaled, diagonal))
             out[1].append(jnp.where(lane <= row + base, scaled, 0.0))
-        if k + 1 == stop and stop < count:
+        if k + 1 == stop and reach < count:
             begin = stop - group
             low, high = ROWS * begin, ROWS * stop
             for X, out in zip(tasks, outs):
                 uppers = jnp.concatenate(out[0][begin:stop], axis=0)
                 lowers = jnp.concatenate(out[1][begin:stop], axis=0)
                 after = lax.broadcasted_iota(jnp.int32, uppers.shape, 1) >= high
-                change = dot_tn(uppers, jnp.where(after, uppers, lowers))
+                change = exact_tn(uppers, jnp.where(after, uppers, lowers))
                 here = (lane >= low) & (lane < high)
-                for j in range(stop, count):
+                for j in range(reach, count):
                     X[j] = jnp.where(here, 0.0, X[j]) - change[ROWS * j : ROWS * (j + 1)]
     return [(jnp.concatenate(u, axis=0), jnp.concatenate(v, axis=0)) for u, v in outs]
 
@@ -159,7 +238,7 @@
         for m, U, L in zip(matrices, uppers, lowers):
             head = cut(m, j, j)
             for k in range(j):
-                head = head - dot_nt(L[j, k], L[j, k])
+                head = head - exact_nt(L[j, k], L[j, k])
             heads.append(head)
         for m, U, L, V, (u, v) in zip(
             matrices, uppers, lowers, inverses, factor_small(heads, board, GROUP)
@@ -170,18 +249,18 @@
                 right = cut(m, j, i)
                 down = cut(m, i, j)
                 for k in range(j):
-                    right = right - dot_nn(L[j, k], U[k, i])
-                    down = down - dot_nn(L[i, k], U[k, j])
-                U[j, i] = dot_nn(v, right)
-                L[i, j] = dot_nt(down, v)
+                    right = right - exact_nn(L[j, k], U[k, i])
+                    down = down - exact_nn(L[i, k], U[k, j])
+                U[j, i] = exact_nn(v, right)
+                L[i, j] = exact_nt(down, v)
     outs = []
     for U, L, V in zip(uppers, lowers, inverses):
         for i in range(blocks):
             for j in range(i):
-                total = dot_nn(L[i, j], V[j, j])
+                total = exact_nn(L[i, j], V[j, j])
                 for k in range(j + 1, i):
-                    total = total + dot_nn(L[i, k], V[k, j])
-                V[i, j] = -dot_nn(V[i, i], total)
+                    total = total + exact_nn(L[i, k], V[k, j])
+                V[i, j] = -exact_nn(V[i, i], total)
         whole = [
             jnp.concatenate(
                 [
@@ -203,17 +282,19 @@
 
 
 def first_of(values):
-    row = lax.broadcasted_iota(jnp.int32, (ROWS, values.shape[1]), 0)
+    row = lax.broadcasted_iota(jnp.int32, (VECTOR, values.shape[1]), 0)
     return jnp.where(row == 0, values, 0.0)
 
 
-def maps_kernel(transition_ref, sensing_ref, noise_ref, maps_ref, consts_ref):
+def maps_kernel(transition_ref, sensing_ref, noise_ref, left_ref, right_ref, consts_ref):
     n = transition_ref.shape[0]
     transition = transition_ref[...]
     sensing = sensing_ref[...]
     noise = noise_ref[...]
-    maps_ref[0:n] = transition
-    maps_ref[n:] = dot_nn(sensing, transition)
+    maps = jnp.concatenate([transition, dot_nn(sensing, transition)], axis=0)
+    high, low, least = pieces(maps, 3)
+    left_ref[...] = jnp.concatenate([high, low, least, high], axis=1)
+    right_ref[...] = jnp.concatenate([high, high, low, least], axis=1)
     noise_sensed = dot_nt(noise, sensing)
     consts_ref[0:n, 0:n] = noise
     consts_ref[0:n, n:] = noise_sensed
@@ -226,7 +307,8 @@
     times,
     begin_ref,
     rows_ref,
-    maps_ref,
+    left_ref,
+    right_ref,
     consts_ref,
     mean_ref,
     prior_ref,
@@ -239,7 +321,7 @@
     board,
 ):
     n = prior_ref.shape[0]
-    o = maps_ref.shape[0] - n
+    o = left_ref.shape[0] - n
     begin = begin_ref[0]
     eye_sense = unit(o)
 
@@ -255,20 +337,24 @@
 
     moved_ref[0:n] = jnp.zeros((n, n), jnp.float32)
     moved_ref[n : 2 * n] = unit(n)
-    moved_ref[2 * n :] = jnp.zeros((ROWS, n), jnp.float32)
+    moved_ref[2 * n :] = jnp.zeros((VECTOR, n), jnp.float32)
     waiting_ref[...] = jnp.zeros_like(waiting_ref)
     inverse_ref[...] = jnp.zeros_like(inverse_ref)
     info_ref[...] = jnp.zeros_like(info_ref)
-    sensed = maps_ref[n:]
-    fresh = begin == 0
+
+    def through_sensed(spread):
+        half = join_nt(left_moving(spread), right_ref[n:])
+        return join_nn(left_ref[n:], right_moving(half))
+
     sensed_ref[...] = first_spread(
-        0, jnp.where(fresh, dot_nn(sensed, dot_nt(prior_ref[...], sensed)), 0.0)
+        0, jnp.where(begin == 0, through_sensed(prior_ref[...]), 0.0)
     )
 
     def update():
-        white = dot_nt(waiting_ref[...], inverse_ref[...])
-        info_ref[...] = info_ref[...] + dot_nt(white[n:], white[n : 2 * n])
-        return moved_ref[...] - dot_nt(white, white[0:n])
+        white = join_nt(waiting_ref[...], inverse_ref[...])
+        left = left_of(white)
+        info_ref[...] = info_ref[...] + join_nt(left[n:], right_of(white[n : 2 * n]))
+        return moved_ref[...] - join_nt(left, right_of(white[0:n]))
 
     def step(k, carry):
         ((_, inverse),) = factor_small([sensed_ref[...]], board, o // ROWS)
@@ -282,19 +368,18 @@
             ),
             state,
         )
-        moved = dot_nt(state, maps_ref[...])
-        ahead = dot_nn(maps_ref[0:n], moved[0:n]) + consts_ref[0:n]
+        moved = join_nt(left_moving(state), right_ref[...])
+        ahead = join_nn(left_ref[0:n], right_moving(moved[0:n])) + consts_ref[0:n]
         moved_ref[0:n] = ahead[:, 0:n]
         moved_ref[n:] = moved[n:, 0:n]
-        waiting_ref[0:n] = ahead[:, n:]
-        waiting_ref[n : 2 * n] = moved[n : 2 * n, n:]
-        waiting_ref[2 * n :] = moved[2 * n :, n:] - first_of(line_at(k)[:, 0:o])
-        spread = jnp.where(later == 0, prior_ref[...], ahead[:, 0:n])
-        kept = dot_nn(maps_ref[n:], dot_nt(spread, maps_ref[n:]))
-        gained = dot_nt(dot_nn(maps_ref[n:], ahead[:, n:]), inverse)
+        waiting_ref[0:n] = left_of(ahead[:, n:])
+        waiting_ref[n : 2 * n] = left_of(moved[n : 2 * n, n:])
+        waiting_ref[2 * n :] = left_of(moved[2 * n :, n:] - first_of(line_at(k)[:, 0:o]))
+        kept = through_sensed(jnp.where(later == 0, prior_ref[...], ahead[:, 0:n]))
+        gained = exact_nt(join_nn(left_ref[n:], right_moving(ahead[:, n:])), inverse)
         gained = jnp.where(later == 0, 0.0, gained)
-        sensed_ref[...] = first_spread(k + 1, kept - dot_nt(gained, gained))
-        inverse_ref[...] = inverse
+        sensed_ref[...] = first_spread(k + 1, kept - exact_nt(gained, gained))
+        inverse_ref[...] = right_of(inverse)
         return carry
 
     lax.fori_loop(0, steps, step, 0)
@@ -314,8 +399,8 @@
     def of_middle(rows, near, far):
         return jnp.where(late, near[rows], far[rows])
 
-    spread_rows, move_rows, center_rows = slice(0, n), slice(n, 2 * n), slice(2 * n, 2 * n + ROWS)
-    info_rows, vector_rows = slice(0, n), slice(n, n + ROWS)
+    spread_rows, move_rows, center_rows = slice(0, n), slice(n, 2 * n), slice(2 * n, 2 * n + VECTOR)
+    info_rows, vector_rows = slice(0, n), slice(n, n + VECTOR)
     cut_spread = of_cut(spread_rows, state_ref, far_state_ref)
     cut_center = of_cut(center_rows, state_ref, far_state_ref)
     cut_info = of_cut(info_rows, info_ref, far_info_ref)
@@ -327,30 +412,30 @@
     mid_vector = of_middle(vector_rows, info_ref, far_info_ref)
 
     (mid_root, _), (cut_root, _) = factor([mid_spread, cut_spread], board)
-    rooted = dot_nt(cut_info, mid_root)
-    ((_, inner),) = factor([eye + dot_nn(mid_root, rooted)], board)
-    carried = dot_nn(inner, mid_root)
-    mixing = dot_nt(rooted, inner)
-    kept = cut_info - dot_nt(mixing, mixing)
-    early_info = mid_info + dot_nt(dot_nn(move, kept), move)
+    rooted = exact_nt(cut_info, mid_root)
+    ((_, inner),) = factor([eye + exact_nn(mid_root, rooted)], board)
+    carried = near_nn(inner, mid_root)
+    mixing = near_nt(rooted, inner)
+    kept = cut_info - near_nt(mixing, mixing)
+    early_info = mid_info + near_nt(near_nn(move, kept), move)
     ((_, last),) = factor(
-        [eye + dot_nn(cut_root, dot_nt(early_info, cut_root))], board
-    )
-    residue = -cut_vector - dot_nn(mid_center, cut_info)
-    residue_carried = dot_nt(residue, carried)
-    early_vector = dot_nt(residue - dot_nt(residue_carried, mixing), move) - mid_vector
-    pull = early_vector - dot_nn(cut_center, early_info)
+        [eye + exact_nn(cut_root, exact_nt(early_info, cut_root))], board
+    )
+    residue = -cut_vector - near_nn(mid_center, cut_info)
+    residue_carried = near_nt(residue, carried)
+    early_vector = near_nt(residue - near_nt(residue_carried, mixing), move) - mid_vector
+    pull = early_vector - near_nn(cut_center, early_info)
     cut_root_t = cut_root.T
-    through = move - dot_nn(dot_nn(move, mixing), carried)
-    through_center = mid_center + dot_nn(residue_carried, carried)
+    through = move - near_nn(near_nn(move, mixing), carried)
+    through_center = mid_center + near_nn(residue_carried, carried)
     carried_t = carried.T
-    leftover = dot_nt(carried_t, carried_t)
-    late_root = dot_nt(through.T, cut_root)
-    early_root = dot_nt(cut_root_t, last)
-    early_center = cut_center + dot_nt(dot_nn(pull, early_root), early_root)
-    root = dot_nt(jnp.where(late, late_root, cut_root_t), last)
-    cov_ref[0] = jnp.where(late, leftover, 0.0) + dot_nt(root, root)
-    late_center = dot_nn(early_center, through) + through_center
+    leftover = near_nt(carried_t, carried_t)
+    late_root = near_nt(through.T, cut_root)
+    early_root = near_nt(cut_root_t, last)
+    early_center = cut_center + near_nt(near_nn(pull, early_root), early_root)
+    root = near_nt(jnp.where(late, late_root, cut_root_t), last)
+    cov_ref[0] = jnp.where(late, leftover, 0.0) + near_nt(root, root)
+    late_center = near_nn(early_center, through) + through_center
     mean_ref[...] = jnp.where(late, late_center, early_center)[0:1]
 
 
@@ -404,27 +489,28 @@
     def shape(*dims):
         return jax.ShapeDtypeStruct(dims, jnp.float32)
 
-    maps, consts = pl.pallas_call(
+    passes = jax.ShapeDtypeStruct((n + o, 4 * n), jnp.bfloat16)
+    left, right, consts = pl.pallas_call(
         maps_kernel,
-        out_shape=(shape(n + o, n), shape(n + o, n + o)),
+        out_shape=(passes, passes, shape(n + o, n + o)),
         in_specs=[vmem] * 3,
-        out_specs=(vmem, vmem),
+        out_specs=(vmem, vmem, vmem),
         compiler_params=params,
     )(transition, sensing, process_noise)
     state, info = pl.pallas_call(
         functools.partial(window_kernel, half, devices),
-        out_shape=(shape(2 * n + ROWS, n), shape(n + ROWS, n)),
-        in_specs=[smem] + [vmem] * 5,
+        out_shape=(shape(2 * n + VECTOR, n), shape(n + VECTOR, n)),
+        in_specs=[smem] + [vmem] * 6,
         out_specs=(vmem, vmem),
         scratch_shapes=[
-            pltpu.VMEM((2 * n + ROWS, n), jnp.float32),
-            pltpu.VMEM((2 * n + ROWS, o), jnp.float32),
-            pltpu.VMEM((o, o), jnp.float32),
+            pltpu.VMEM((2 * n + VECTOR, n), jnp.float32),
+            pltpu.VMEM((2 * n + VECTOR, 3 * o), jnp.bfloat16),
+            pltpu.VMEM((o, 3 * o), jnp.bfloat16),
             pltpu.VMEM((o, o), jnp.float32),
             pltpu.VMEM((1, 2, BOARD, o), jnp.float32),
         ],
         compiler_params=params,
-    )(begin.reshape(1), rows, maps, consts, prior_mean.reshape(1, n), prior_covariance)
+    )(begin.reshape(1), rows, left, right, consts, prior_mean.reshape(1, n), prior_covariance)
     swap = [(i, i ^ 1) for i in range(devices)]
     far_state = lax.ppermute(state, "tm", swap)
     far_info = lax.ppermute(info, "tm", swap)

time: 169 us -> 159 us (0.941)
  Pallas kernels: 132 us -> 122 us
    pallas_call x1, Pallas kernels: 93.2 us -> 87 us  [shards(): pl.pallas_call(functools.partial(window_kernel, half, devices), out_shape...]
    pallas_call x1, Pallas kernels: 37.4 us -> 33.9 us  [shards(): pl.pallas_call(meet_kernel, out_shape=(shape(1, n), shape(1, n, n)), in_s...]
where the time goes in v1:
time: 159 us
  Pallas kernels  122 us (77%)
  starting transfers between devices  23.9 us (15%)
  waiting for transfers between devices  6.87 us (4%)
  local copies, waits for them, and re-layouts  5.46 us (3%)
    pallas_call x1, Pallas kernels, shards(): pl.pallas_call(functools.partial(window_kernel, half, devices), out_shape...  87 us
    pallas_call x1, Pallas kernels, shards(): pl.pallas_call(meet_kernel, out_shape=(shape(1, n), shape(1, n, n)), in_s...  33.9 us
    ppermute x4, starting transfers between devices, gather_rows(): lax.ppermute(rows, axis, [((begins[i] + j) % devices, i) for i in range(d...  8.93 us
    ppermute x3, starting transfers between devices, gather_rows(): parts.append(lax.ppermute(rows[:size], axis, pairs))  7.98 us
    ppermute x2, starting transfers between devices, shards(): return (lax.ppermute(mean, 'tm', home), lax.ppermute(cov, 'tm', home))  6.46 us
    unnamed x15, local copies, waits for them, and re-layouts  5.41 us
    ppermute x2, waiting for transfers between devices, shards(): return (lax.ppermute(mean, 'tm', home), lax.ppermute(cov, 'tm', home))  4.98 us
  transfers between devices with their start and end apart: 11, of which 2 were waited for; matrix products, arithmetic and copies ran while one was open for 0% of the time, Pallas kernels for 1%

profile of v1, /device:TPU:1, one launch (start us, length us, event | category | flops | bytes accessed | tf_op | source)
XLA Modules:
  0.0 158.8 jit_solution(3884894347888739022)
XLA Ops:
  0.6 0.0 copy-start.5
  0.6 0.7 constant_dynamic-update-slice_fusion.1
  1.3 0.0 copy-done.5
  1.3 5.7 %collective-permute-start.3 = (f32[1,256]{1,0:T(1,128)S(1)}, f32[1,256]{1,0:T(1,128)S(1)}, u32[]{:S(2)}, u32[]{:S(2)}) collective-permute-start(f32[1,256]{1,0:T(1,128)S(1)} %constant_dynamic-update-slice_fusion), channel_id=1, source_target_pairs={{20,0},{4,1},{22,2},{6,3},{24,4},{8,5},{26,6},{10,7},{28,8},{12,9}... | collective-permute-start | bytes 3080 | tf_op jit(solution)/shard_map/ppermute | solution.py:457
  7.0 0.0 collective-permute-start.2
  7.0 2.6 %collective-permute-start.1 = (f32[1,256]{1,0:T(1,128)S(1)}, f32[1,256]{1,0:T(1,128)S(1)}, u32[]{:S(2)}, u32[]{:S(2)}) collective-permute-start(f32[1,256]{1,0:T(1,128)S(1)} %constant_dynamic-update-slice_fusion), channel_id=1, source_target_pairs={{18,0},{2,1},{20,2},{4,3},{22,4},{6,5},{24,6},{8,7},{26,8},{10,9},... | collective-permute-start | bytes 3080 | tf_op jit(solution)/shard_map/ppermute | solution.py:457
  9.6 0.6 collective-permute-start
  10.3 0.0 collective-permute-done.3
  10.3 0.0 collective-permute-done.2
  10.3 0.0 collective-permute-done.1
  10.3 0.0 collective-permute-done
  10.3 5.4 %collective-permute-start.6 = (f32[4,256]{1,0:T(4,128)S(1)}, f32[4,256]{1,0:T(4,128)S(1)}, u32[]{:S(2)}, u32[]{:S(2)}) collective-permute-start(f32[4,256]{1,0:T(4,128)S(1)} %pad_maximum_fusion), channel_id=1, source_target_pairs={{12,0},{13,1},{14,2},{15,3},{1,4},{0,5},{3,6},{2,7},{5,8},{4,9},{7... | collective-permute-start | bytes 12296 | tf_op jit(solution)/shard_map/ppermute | solution.py:467
  15.8 0.0 collective-permute-start.5
  15.8 2.6 %collective-permute-start.4 = (f32[4,256]{1,0:T(4,128)S(1)}, f32[4,256]{1,0:T(4,128)S(1)}, u32[]{:S(2)}, u32[]{:S(2)}) collective-permute-start(f32[4,256]{1,0:T(4,128)S(1)} %pad_maximum_fusion), channel_id=1, source_target_pairs={{4,0},{5,1},{6,2},{7,3},{8,4},{9,5},{10,6},{11,7},{12,8},{13,9},{1... | collective-permute-start | bytes 12296 | tf_op jit(solution)/shard_map/ppermute | solution.py:467
  18.3 0.0 copy-start.1
  18.3 0.9 copy-done.1
  19.3 0.0 copy-start.2
  19.3 0.9 copy-done.2
  20.2 0.0 copy-start.3
  20.2 0.9 copy-done.3
  21.1 0.0 copy-start
  21.1 0.9 shard_map.86
  22.1 0.0 collective-permute-done.6
  22.1 0.0 collective-permute-done.5
  22.1 0.0 collective-permute-done.4
  22.1 0.0 copy-start.4
  22.1 0.0 copy-done
  22.1 0.7 copy-done.4
  22.8 87.0 %shard_map.87 = (f32[528,256]{1,0:T(8,128)S(1)}, f32[272,256]{1,0:T(8,128)S(1)}) custom-call(s32[1]{0:T(128)} %bitcast.1.begin_ref, f32[16,256]{1,0:T(8,128)S(1)} %concatenate.12.rows_ref, bf16[384,1024]{1,0:T(8,128)(2,1)S(1)} %get-tuple-element.9.left_ref, bf16[384,1024]{1,0:T(8,128)(2,1)S(1)} %get-tuple-element.10.right_ref, ...), custom_call_target="tpu_custom_call" | custom-call | tf_op jit(solution)/shard_map/pallas_call | solution.py:500
  109.8 0.1 collective-permute-start.7
  109.9 0.5 collective-permute-start.8
  110.4 1.8 %collective-permute-done.8.far_info_ref = f32[272,256]{1,0:T(8,128)S(1)} collective-permute-done((f32[272,256]{1,0:T(8,128)S(1)}, f32[272,256]{1,0:T(8,128)S(1)}, u32[]{:S(2)}, u32[]{:S(2)}) %collective-permute-start.8) | collective-permute-done | bytes 278560 | tf_op jit(solution)/shard_map/ppermute | solution.py:516
  112.2 0.0 collective-permute-done.7.far_state_ref
  112.2 33.9 %shard_map.88 = (f32[1,256]{1,0:T(1,128)S(1)}, f32[1,256,256]{2,1,0:T(8,128)S(1)}) custom-call(s32[1]{0:T(128)} %bitcast.role_ref, f32[528,256]{1,0:T(8,128)S(1)} %get-tuple-element.12.state_ref, f32[272,256]{1,0:T(8,128)S(1)} %get-tuple-element.13.info_ref, f32[528,256]{1,0:T(8,128)S(1)} %collective-permute-done.7.far_state_ref, ...), custom_call_target="tpu_custom_call" | custom-call | tf_op jit(solution)/shard_map/pallas_call | solution.py:517
  146.1 4.4 %collective-permute-start.10 = (f32[1,256,256]{2,1,0:T(8,128)S(1)}, f32[1,256,256]{2,1,0:T(8,128)S(1)}, u32[]{:S(2)}, u32[]{:S(2)}) collective-permute-start(f32[1,256,256]{2,1,0:T(8,128)S(1)} %get-tuple-element.15), channel_id=1, source_target_pairs={{0,0},{1,16},{2,2},{3,18},{4,4},{5,20},{6,6},{7,22},{8,8},{9,24},{... | collective-permute-start | bytes 786440 | tf_op jit(solution)/shard_map/ppermute | solution.py:530
  150.5 2.1 %collective-permute-start.9 = (f32[1,256]{1,0:T(1,128)S(1)}, f32[1,256]{1,0:T(1,128)S(1)}, u32[]{:S(2)}, u32[]{:S(2)}) collective-permute-start(f32[1,256]{1,0:T(1,128)S(1)} %get-tuple-element.14), channel_id=1, source_target_pairs={{0,0},{1,16},{2,2},{3,18},{4,4},{5,20},{6,6},{7,22},{8,8},{9,24},{... | collective-permute-start | bytes 3080 | tf_op jit(solution)/shard_map/ppermute | solution.py:530
  152.6 5.0 %collective-permute-done.9 = f32[1,256]{1,0:T(1,128)S(1)} collective-permute-done((f32[1,256]{1,0:T(1,128)S(1)}, f32[1,256]{1,0:T(1,128)S(1)}, u32[]{:S(2)}, u32[]{:S(2)}) %collective-permute-start.9) | collective-permute-done | bytes 1056 | tf_op jit(solution)/shard_map/ppermute | solution.py:530
  157.6 0.0 collective-permute-done.10
  157.6 0.6 copy.12
  158.1 0.7 copy.13
  (3 shorter events, 0.1 us)
Async XLA Ops:
  0.6 0.7 copy-start.5
  1.3 8.9 %collective-permute-start.3 = (f32[1,256]{1,0:T(1,128)S(1)}, f32[1,256]{1,0:T(1,128)S(1)}, u32[]{:S(2)}, u32[]{:S(2)}) collective-permute-start(f32[1,256]{1,0:T(1,128)S(1)} %constant_dynamic-update-slice_fusion), channel_id=1, source_target_pairs={{20,0},{4,1},{22,2},{6,3},{24,4},{8,5},{26,6},{10,7},{28,8},{12,9}... | collective-permute-start | bytes 3080 | tf_op jit(solution)/shard_map/ppermute | solution.py:457
  7.0 3.3 %collective-permute-start.2 = (f32[1,256]{1,0:T(1,128)S(1)}, f32[1,256]{1,0:T(1,128)S(1)}, u32[]{:S(2)}, u32[]{:S(2)}) collective-permute-start(f32[1,256]{1,0:T(1,128)S(1)} %constant_dynamic-update-slice_fusion), channel_id=1, source_target_pairs={{19,0},{3,1},{21,2},{5,3},{23,4},{7,5},{25,6},{9,7},{27,8},{11,9},... | collective-permute-start | bytes 3080 | tf_op jit(solution)/shard_map/ppermute | solution.py:457
  7.0 3.3 %collective-permute-start.1 = (f32[1,256]{1,0:T(1,128)S(1)}, f32[1,256]{1,0:T(1,128)S(1)}, u32[]{:S(2)}, u32[]{:S(2)}) collective-permute-start(f32[1,256]{1,0:T(1,128)S(1)} %constant_dynamic-update-slice_fusion), channel_id=1, source_target_pairs={{18,0},{2,1},{20,2},{4,3},{22,4},{6,5},{24,6},{8,7},{26,8},{10,9},... | collective-permute-start | bytes 3080 | tf_op jit(solution)/shard_map/ppermute | solution.py:457
  9.6 0.7 collective-permute-start
  10.3 11.7 %collective-permute-start.6 = (f32[4,256]{1,0:T(4,128)S(1)}, f32[4,256]{1,0:T(4,128)S(1)}, u32[]{:S(2)}, u32[]{:S(2)}) collective-permute-start(f32[4,256]{1,0:T(4,128)S(1)} %pad_maximum_fusion), channel_id=1, source_target_pairs={{12,0},{13,1},{14,2},{15,3},{1,4},{0,5},{3,6},{2,7},{5,8},{4,9},{7... | collective-permute-start | bytes 12296 | tf_op jit(solution)/shard_map/ppermute | solution.py:467
  15.8 6.3 %collective-permute-start.5 = (f32[4,256]{1,0:T(4,128)S(1)}, f32[4,256]{1,0:T(4,128)S(1)}, u32[]{:S(2)}, u32[]{:S(2)}) collective-permute-start(f32[4,256]{1,0:T(4,128)S(1)} %pad_maximum_fusion), channel_id=1, source_target_pairs={{8,0},{9,1},{10,2},{11,3},{12,4},{13,5},{14,6},{15,7},{1,8},{0,9},... | collective-permute-start | bytes 12296 | tf_op jit(solution)/shard_map/ppermute | solution.py:467
  15.8 6.3 %collective-permute-start.4 = (f32[4,256]{1,0:T(4,128)S(1)}, f32[4,256]{1,0:T(4,128)S(1)}, u32[]{:S(2)}, u32[]{:S(2)}) collective-permute-start(f32[4,256]{1,0:T(4,128)S(1)} %pad_maximum_fusion), channel_id=1, source_target_pairs={{4,0},{5,1},{6,2},{7,3},{8,4},{9,5},{10,6},{11,7},{12,8},{13,9},{1... | collective-permute-start | bytes 12296 | tf_op jit(solution)/shard_map/ppermute | solution.py:467
  18.3 0.9 copy-start.1
  19.3 0.9 copy-start.2
  20.2 0.9 copy-start.3
  21.1 1.0 copy-start
  22.1 0.7 copy-start.4
  109.8 2.4 %collective-permute-start.7 = (f32[528,256]{1,0:T(8,128)S(1)}, f32[528,256]{1,0:T(8,128)S(1)}, u32[]{:S(2)}, u32[]{:S(2)}) collective-permute-start(f32[528,256]{1,0:T(8,128)S(1)} %get-tuple-element.12.state_ref), channel_id=1, source_target_pairs={{0,1},{1,0},{2,3},{3,2},{4,5},{5,4},{6,7},{7,6},{8,9},{9,8},{10,11... | collective-permute-start | bytes 1622024 | tf_op jit(solution)/shard_map/ppermute | solution.py:515
  109.9 2.3 %collective-permute-start.8 = (f32[272,256]{1,0:T(8,128)S(1)}, f32[272,256]{1,0:T(8,128)S(1)}, u32[]{:S(2)}, u32[]{:S(2)}) collective-permute-start(f32[272,256]{1,0:T(8,128)S(1)} %get-tuple-element.13.info_ref), channel_id=1, source_target_pairs={{0,1},{1,0},{2,3},{3,2},{4,5},{5,4},{6,7},{7,6},{8,9},{9,8},{10,11... | collective-permute-start | bytes 835592 | tf_op jit(solution)/shard_map/ppermute | solution.py:516
  146.1 11.5 %collective-permute-start.10 = (f32[1,256,256]{2,1,0:T(8,128)S(1)}, f32[1,256,256]{2,1,0:T(8,128)S(1)}, u32[]{:S(2)}, u32[]{:S(2)}) collective-permute-start(f32[1,256,256]{2,1,0:T(8,128)S(1)} %get-tuple-element.15), channel_id=1, source_target_pairs={{0,0},{1,16},{2,2},{3,18},{4,4},{5,20},{6,6},{7,22},{8,8},{9,24},{... | collective-permute-start | bytes 786440 | tf_op jit(solution)/shard_map/ppermute | solution.py:530
  150.5 7.1 %collective-permute-start.9 = (f32[1,256]{1,0:T(1,128)S(1)}, f32[1,256]{1,0:T(1,128)S(1)}, u32[]{:S(2)}, u32[]{:S(2)}) collective-permute-start(f32[1,256]{1,0:T(1,128)S(1)} %get-tuple-element.14), channel_id=1, source_target_pairs={{0,0},{1,16},{2,2},{3,18},{4,4},{5,20},{6,6},{7,22},{8,8},{9,24},{... | collective-permute-start | bytes 3080 | tf_op jit(solution)/shard_map/ppermute | solution.py:530

commit v2 on v1

--- a/solution.py
+++ b/solution.py
@@ -9,8 +9,6 @@
 
 ROWS = 8
 LANES = 128
-GROUP = 4
-LEAD = 1
 VECTOR = 16
 EXTRA = ROWS + ROWS // 2
 BOARD = ROWS * (EXTRA + ROWS)
@@ -81,17 +79,6 @@
     return jnp.broadcast_to(x[:, lane : lane + 1], x.shape)
 
 
-def exact_tn(left, right):
-    a, b, c = pieces(left, 3)
-    p, q, r = pieces(right, 3)
-    return lax.dot_general(
-        jnp.concatenate([a, a, b, a, b, c], axis=0),
-        jnp.concatenate([p, q, p, r, q, p], axis=0),
-        (((0,), (0,)), ((), ())),
-        preferred_element_type=jnp.float32,
-    )
-
-
 def exact_nt(left, right):
     a, b, c = pieces(left, 3)
     p, q, r = pieces(right, 3)
@@ -117,10 +104,9 @@
     return join_nt(left_of(left), right_of(right))
 
 
-def factor_small(matrices, board, group):
+def factor_small(matrices, board):
     side = matrices[0].shape[0]
     count = side // ROWS
-    group = min(group, count)
     shape = (ROWS, side)
     row = lax.broadcasted_iota(jnp.int32, shape, 0)
     lane = lax.broadcasted_iota(jnp.int32, shape, 1)
@@ -130,8 +116,6 @@
     for k in range(count):
         base = ROWS * k
         more = k + 1 < count
-        stop = min(count, (k // group + 1) * group)
-        reach = min(count, stop + LEAD)
         for t, (X, out) in enumerate(zip(tasks, outs)):
 
             def put(slot, values):
@@ -173,6 +157,8 @@
                 xq = spread(ROWS + i // 2, i + 1)
                 xq = jnp.where(lane == p + 1, 1.0, jnp.where(lane == p, 0.0, xq))
                 xq = xq - ratio * xp
+                xp_scaled = xp * ra
+                xq_scaled = xq * (a * rdet)
                 Z = jnp.where((row == i) & (lane == p), 1.0, X[k])
                 if i + 2 < ROWS:
                     f0 = cols[i] * ra
@@ -183,48 +169,36 @@
                     m1 = jnp.where(row > i + 1, f1, 0.0)
                     Z = jnp.where((row > i + 1) & pair, 0.0, Z) - m0 * xp - m1 * xq
                 X[k] = jnp.where(row == i + 1, xq, Z)
-                for j in range(k + 1, reach):
-                    if j == k + 1:
-                        g0, g1 = nexts[i], nexts[i + 1]
-                    else:
-                        g0 = spread_lane(X[j], p)
-                        g1 = spread_lane(X[j], p + 1)
+                if more:
+                    g0, g1 = nexts[i], nexts[i + 1]
                     h0 = g0 * ra
                     g1 = a * g1 - b * g0
                     h1 = g1 * rdet
-                    if j == k + 1:
-                        put(EXTRA + i, g0)
-                        put(EXTRA + i + 1, g1 * ra)
-                        for q in range(ROWS):
-                            first, second = spread(EXTRA + i, q), spread(EXTRA + i + 1, q)
-                            heads[t][q] = heads[t][q] - h0 * first - h1 * second
-                        for q in rest:
-                            nexts[q] = nexts[q] - h0 * firsts[q] - h1 * seconds[q]
-                    X[j] = jnp.where(pair, 0.0, X[j]) - h0 * xp - h1 * xq
+                    put(EXTRA + i, g0)
+                    put(EXTRA + i + 1, g1 * ra)
+                    for q in range(ROWS):
+                        first, second = spread(EXTRA + i, q), spread(EXTRA + i + 1, q)
+                        heads[t][q] = heads[t][q] - h0 * first - h1 * second
+                    for q in rest:
+                        nexts[q] = nexts[q] - h0 * firsts[q] - h1 * seconds[q]
+                    X[k + 1] = jnp.where(pair, 0.0, X[k + 1]) - h0 * xp - h1 * xq
+                for j in range(k + 2, count):
+                    g0 = spread_lane(X[j], p)
+                    g1 = spread_lane(X[j], p + 1) - ratio * g0
+                    X[j] = jnp.where(pair, 0.0, X[j]) - g0 * xp_scaled - g1 * xq_scaled
             s = lax.rsqrt(pivots)
             s = s * (1.5 - 0.5 * pivots * s * s)
             scaled = X[k] * s
             diagonal = jnp.where(lane == row + base, pivots * s, 0.0)
             out[0].append(jnp.where(lane > row + base, scaled, diagonal))
             out[1].append(jnp.where(lane <= row + base, scaled, 0.0))
-        if k + 1 == stop and reach < count:
-            begin = stop - group
-            low, high = ROWS * begin, ROWS * stop
-            for X, out in zip(tasks, outs):
-                uppers = jnp.concatenate(out[0][begin:stop], axis=0)
-                lowers = jnp.concatenate(out[1][begin:stop], axis=0)
-                after = lax.broadcasted_iota(jnp.int32, uppers.shape, 1) >= high
-                change = exact_tn(uppers, jnp.where(after, uppers, lowers))
-                here = (lane >= low) & (lane < high)
-                for j in range(reach, count):
-                    X[j] = jnp.where(here, 0.0, X[j]) - change[ROWS * j : ROWS * (j + 1)]
     return [(jnp.concatenate(u, axis=0), jnp.concatenate(v, axis=0)) for u, v in outs]
 
 
 def factor(matrices, board):
     blocks = matrices[0].shape[0] // LANES
     if blocks == 1:
-        return factor_small(matrices, board, GROUP)
+        return factor_small(matrices, board)
 
     def cut(m, i, j):
         return m[LANES * i : LANES * (i + 1), LANES * j : LANES * (j + 1)]
@@ -241,7 +215,7 @@
                 head = head - exact_nt(L[j, k], L[j, k])
             heads.append(head)
         for m, U, L, V, (u, v) in zip(
-            matrices, uppers, lowers, inverses, factor_small(heads, board, GROUP)
+            matrices, uppers, lowers, inverses, factor_small(heads, board)
         ):
             U[j, j] = u
             V[j, j] = v
@@ -357,7 +331,7 @@
         return moved_ref[...] - join_nt(left, right_of(white[0:n]))
 
     def step(k, carry):
-        ((_, inverse),) = factor_small([sensed_ref[...]], board, o // ROWS)
+        ((_, inverse),) = factor_small([sensed_ref[...]], board)
         now = wrap(begin + k)
         later = wrap(now + 1)
         state = update()
@@ -383,7 +357,10 @@
         return carry
 
     lax.fori_loop(0, steps, step, 0)
-    state_ref[...] = update()
+    state = update()
+    ((root, _),) = factor([state[0:n]], board)
+    state_ref[0:n] = root
+    state_ref[n:] = state[n:]
 
 
 def meet_kernel(
@@ -399,19 +376,18 @@
     def of_middle(rows, near, far):
         return jnp.where(late, near[rows], far[rows])
 
-    spread_rows, move_rows, center_rows = slice(0, n), slice(n, 2 * n), slice(2 * n, 2 * n + VECTOR)
+    root_rows, move_rows, center_rows = slice(0, n), slice(n, 2 * n), slice(2 * n, 2 * n + VECTOR)
     info_rows, vector_rows = slice(0, n), slice(n, n + VECTOR)
-    cut_spread = of_cut(spread_rows, state_ref, far_state_ref)
+    cut_root = of_cut(root_rows, state_ref, far_state_ref)
     cut_center = of_cut(center_rows, state_ref, far_state_ref)
     cut_info = of_cut(info_rows, info_ref, far_info_ref)
     cut_vector = of_cut(vector_rows, info_ref, far_info_ref)
-    mid_spread = of_middle(spread_rows, state_ref, far_state_ref)
+    mid_root = of_middle(root_rows, state_ref, far_state_ref)
     move = of_middle(move_rows, state_ref, far_state_ref)
     mid_center = of_middle(center_rows, state_ref, far_state_ref)
     mid_info = of_middle(info_rows, info_ref, far_info_ref)
     mid_vector = of_middle(vector_rows, info_ref, far_info_ref)
 
-    (mid_root, _), (cut_root, _) = factor([mid_spread, cut_spread], board)
     rooted = exact_nt(cut_info, mid_root)
     ((_, inner),) = factor([eye + exact_nn(mid_root, rooted)], board)
     carried = near_nn(inner, mid_root)
@@ -519,7 +495,7 @@
         out_shape=(shape(1, n), shape(1, n, n)),
         in_specs=[smem] + [vmem] * 4,
         out_specs=(vmem, vmem),
-        scratch_shapes=[pltpu.VMEM((2, 2, BOARD, LANES), jnp.float32)],
+        scratch_shapes=[pltpu.VMEM((1, 2, BOARD, LANES), jnp.float32)],
         compiler_params=params,
     )(role.reshape(1), state, info, far_state, far_info)
     home = []

time: 159 us -> 157 us (0.987)
  Pallas kernels: 122 us -> 120 us
    pallas_call x1, Pallas kernels: 33.9 us -> 25.4 us  [shards(): pl.pallas_call(meet_kernel, out_shape=(shape(1, n), shape(1, n, n)), in_s...]
    pallas_call x1, Pallas kernels: 87 us -> 93.7 us  [shards(): pl.pallas_call(functools.partial(window_kernel, half, devices), out_shape...]
where the time goes in v2:
time: 157 us
  Pallas kernels  120 us (76%)
  starting transfers between devices  23.9 us (15%)
  waiting for transfers between devices  6.87 us (4%)
  local copies, waits for them, and re-layouts  5.46 us (3%)
    pallas_call x1, Pallas kernels, shards(): pl.pallas_call(functools.partial(window_kernel, half, devices), out_shape...  93.7 us
    pallas_call x1, Pallas kernels, shards(): pl.pallas_call(meet_kernel, out_shape=(shape(1, n), shape(1, n, n)), in_s...  25.4 us
    ppermute x4, starting transfers between devices, gather_rows(): lax.ppermute(rows, axis, [((begins[i] + j) % devices, i) for i in range(d...  8.93 us
    ppermute x3, starting transfers between devices, gather_rows(): parts.append(lax.ppermute(rows[:size], axis, pairs))  7.98 us
    ppermute x2, starting transfers between devices, shards(): return (lax.ppermute(mean, 'tm', home), lax.ppermute(cov, 'tm', home))  6.46 us
    unnamed x15, local copies, waits for them, and re-layouts  5.41 us
    ppermute x2, waiting for transfers between devices, shards(): return (lax.ppermute(mean, 'tm', home), lax.ppermute(cov, 'tm', home))  4.98 us
  transfers between devices with their start and end apart: 11, of which 2 were waited for; matrix products, arithmetic and copies ran while one was open for 0% of the time, Pallas kernels for 1%

profile of v2, /device:TPU:1, one launch (start us, length us, event | category | flops | bytes accessed | tf_op | source)
XLA Modules:
  0.0 157.1 jit_solution(12102028657602616471)
XLA Ops:
  0.6 0.0 copy-start.5
  0.6 0.7 constant_dynamic-update-slice_fusion.1
  1.3 0.0 copy-done.5
  1.3 5.7 %collective-permute-start.3 = (f32[1,256]{1,0:T(1,128)S(1)}, f32[1,256]{1,0:T(1,128)S(1)}, u32[]{:S(2)}, u32[]{:S(2)}) collective-permute-start(f32[1,256]{1,0:T(1,128)S(1)} %constant_dynamic-update-slice_fusion), channel_id=1, source_target_pairs={{20,0},{4,1},{22,2},{6,3},{24,4},{8,5},{26,6},{10,7},{28,8},{12,9}... | collective-permute-start | bytes 3080 | tf_op jit(solution)/shard_map/ppermute | solution.py:433
  7.0 0.0 collective-permute-start.2
  7.0 2.6 %collective-permute-start.1 = (f32[1,256]{1,0:T(1,128)S(1)}, f32[1,256]{1,0:T(1,128)S(1)}, u32[]{:S(2)}, u32[]{:S(2)}) collective-permute-start(f32[1,256]{1,0:T(1,128)S(1)} %constant_dynamic-update-slice_fusion), channel_id=1, source_target_pairs={{18,0},{2,1},{20,2},{4,3},{22,4},{6,5},{24,6},{8,7},{26,8},{10,9},... | collective-permute-start | bytes 3080 | tf_op jit(solution)/shard_map/ppermute | solution.py:433
  9.6 0.6 collective-permute-start
  10.3 0.0 collective-permute-done.3
  10.3 0.0 collective-permute-done.2
  10.3 0.0 collective-permute-done.1
  10.3 0.0 collective-permute-done
  10.3 5.4 %collective-permute-start.6 = (f32[4,256]{1,0:T(4,128)S(1)}, f32[4,256]{1,0:T(4,128)S(1)}, u32[]{:S(2)}, u32[]{:S(2)}) collective-permute-start(f32[4,256]{1,0:T(4,128)S(1)} %pad_maximum_fusion), channel_id=1, source_target_pairs={{12,0},{13,1},{14,2},{15,3},{1,4},{0,5},{3,6},{2,7},{5,8},{4,9},{7... | collective-permute-start | bytes 12296 | tf_op jit(solution)/shard_map/ppermute | solution.py:443
  15.8 0.0 collective-permute-start.5
  15.8 2.6 %collective-permute-start.4 = (f32[4,256]{1,0:T(4,128)S(1)}, f32[4,256]{1,0:T(4,128)S(1)}, u32[]{:S(2)}, u32[]{:S(2)}) collective-permute-start(f32[4,256]{1,0:T(4,128)S(1)} %pad_maximum_fusion), channel_id=1, source_target_pairs={{4,0},{5,1},{6,2},{7,3},{8,4},{9,5},{10,6},{11,7},{12,8},{13,9},{1... | collective-permute-start | bytes 12296 | tf_op jit(solution)/shard_map/ppermute | solution.py:443
  18.3 0.0 copy-start.1
  18.3 0.9 copy-done.1
  19.3 0.0 copy-start.2
  19.3 0.9 copy-done.2
  20.2 0.0 copy-start.3
  20.2 0.9 copy-done.3
  21.1 0.0 copy-start
  21.1 0.9 shard_map.86
  22.1 0.0 collective-permute-done.6
  22.1 0.0 collective-permute-done.5
  22.1 0.0 collective-permute-done.4
  22.1 0.0 copy-start.4
  22.1 0.0 copy-done
  22.1 0.7 copy-done.4
  22.8 93.7 %shard_map.87 = (f32[528,256]{1,0:T(8,128)S(1)}, f32[272,256]{1,0:T(8,128)S(1)}) custom-call(s32[1]{0:T(128)} %bitcast.1.begin_ref, f32[16,256]{1,0:T(8,128)S(1)} %concatenate.12.rows_ref, bf16[384,1024]{1,0:T(8,128)(2,1)S(1)} %get-tuple-element.9.left_ref, bf16[384,1024]{1,0:T(8,128)(2,1)S(1)} %get-tuple-element.10.right_ref, ...), custom_call_target="tpu_custom_call" | custom-call | tf_op jit(solution)/shard_map/pallas_call | solution.py:476
  116.5 0.1 collective-permute-start.7
  116.6 0.5 collective-permute-start.8
  117.1 1.8 %collective-permute-done.8.far_info_ref = f32[272,256]{1,0:T(8,128)S(1)} collective-permute-done((f32[272,256]{1,0:T(8,128)S(1)}, f32[272,256]{1,0:T(8,128)S(1)}, u32[]{:S(2)}, u32[]{:S(2)}) %collective-permute-start.8) | collective-permute-done | bytes 278560 | tf_op jit(solution)/shard_map/ppermute | solution.py:492
  118.9 0.0 collective-permute-done.7.far_state_ref
  118.9 25.4 %shard_map.88 = (f32[1,256]{1,0:T(1,128)S(1)}, f32[1,256,256]{2,1,0:T(8,128)S(1)}) custom-call(s32[1]{0:T(128)} %bitcast.role_ref, f32[528,256]{1,0:T(8,128)S(1)} %get-tuple-element.12.state_ref, f32[272,256]{1,0:T(8,128)S(1)} %get-tuple-element.13.info_ref, f32[528,256]{1,0:T(8,128)S(1)} %collective-permute-done.7.far_state_ref, ...), custom_call_target="tpu_custom_call" | custom-call | tf_op jit(solution)/shard_map/pallas_call | solution.py:493
  144.4 4.4 %collective-permute-start.10 = (f32[1,256,256]{2,1,0:T(8,128)S(1)}, f32[1,256,256]{2,1,0:T(8,128)S(1)}, u32[]{:S(2)}, u32[]{:S(2)}) collective-permute-start(f32[1,256,256]{2,1,0:T(8,128)S(1)} %get-tuple-element.15), channel_id=1, source_target_pairs={{0,0},{1,16},{2,2},{3,18},{4,4},{5,20},{6,6},{7,22},{8,8},{9,24},{... | collective-permute-start | bytes 786440 | tf_op jit(solution)/shard_map/ppermute | solution.py:506
  148.8 2.1 %collective-permute-start.9 = (f32[1,256]{1,0:T(1,128)S(1)}, f32[1,256]{1,0:T(1,128)S(1)}, u32[]{:S(2)}, u32[]{:S(2)}) collective-permute-start(f32[1,256]{1,0:T(1,128)S(1)} %get-tuple-element.14), channel_id=1, source_target_pairs={{0,0},{1,16},{2,2},{3,18},{4,4},{5,20},{6,6},{7,22},{8,8},{9,24},{... | collective-permute-start | bytes 3080 | tf_op jit(solution)/shard_map/ppermute | solution.py:506
  150.9 5.0 %collective-permute-done.9 = f32[1,256]{1,0:T(1,128)S(1)} collective-permute-done((f32[1,256]{1,0:T(1,128)S(1)}, f32[1,256]{1,0:T(1,128)S(1)}, u32[]{:S(2)}, u32[]{:S(2)}) %collective-permute-start.9) | collective-permute-done | bytes 1056 | tf_op jit(solution)/shard_map/ppermute | solution.py:506
  155.8 0.0 collective-permute-done.10
  155.8 0.6 copy.12
  156.4 0.7 copy.13
  (3 shorter events, 0.1 us)
Async XLA Ops:
  0.6 0.7 copy-start.5
  1.3 8.9 %collective-permute-start.3 = (f32[1,256]{1,0:T(1,128)S(1)}, f32[1,256]{1,0:T(1,128)S(1)}, u32[]{:S(2)}, u32[]{:S(2)}) collective-permute-start(f32[1,256]{1,0:T(1,128)S(1)} %constant_dynamic-update-slice_fusion), channel_id=1, source_target_pairs={{20,0},{4,1},{22,2},{6,3},{24,4},{8,5},{26,6},{10,7},{28,8},{12,9}... | collective-permute-start | bytes 3080 | tf_op jit(solution)/shard_map/ppermute | solution.py:433
  7.0 3.3 %collective-permute-start.2 = (f32[1,256]{1,0:T(1,128)S(1)}, f32[1,256]{1,0:T(1,128)S(1)}, u32[]{:S(2)}, u32[]{:S(2)}) collective-permute-start(f32[1,256]{1,0:T(1,128)S(1)} %constant_dynamic-update-slice_fusion), channel_id=1, source_target_pairs={{19,0},{3,1},{21,2},{5,3},{23,4},{7,5},{25,6},{9,7},{27,8},{11,9},... | collective-permute-start | bytes 3080 | tf_op jit(solution)/shard_map/ppermute | solution.py:433
  7.0 3.3 %collective-permute-start.1 = (f32[1,256]{1,0:T(1,128)S(1)}, f32[1,256]{1,0:T(1,128)S(1)}, u32[]{:S(2)}, u32[]{:S(2)}) collective-permute-start(f32[1,256]{1,0:T(1,128)S(1)} %constant_dynamic-update-slice_fusion), channel_id=1, source_target_pairs={{18,0},{2,1},{20,2},{4,3},{22,4},{6,5},{24,6},{8,7},{26,8},{10,9},... | collective-permute-start | bytes 3080 | tf_op jit(solution)/shard_map/ppermute | solution.py:433
  9.6 0.7 collective-permute-start
  10.3 11.7 %collective-permute-start.6 = (f32[4,256]{1,0:T(4,128)S(1)}, f32[4,256]{1,0:T(4,128)S(1)}, u32[]{:S(2)}, u32[]{:S(2)}) collective-permute-start(f32[4,256]{1,0:T(4,128)S(1)} %pad_maximum_fusion), channel_id=1, source_target_pairs={{12,0},{13,1},{14,2},{15,3},{1,4},{0,5},{3,6},{2,7},{5,8},{4,9},{7... | collective-permute-start | bytes 12296 | tf_op jit(solution)/shard_map/ppermute | solution.py:443
  15.8 6.3 %collective-permute-start.5 = (f32[4,256]{1,0:T(4,128)S(1)}, f32[4,256]{1,0:T(4,128)S(1)}, u32[]{:S(2)}, u32[]{:S(2)}) collective-permute-start(f32[4,256]{1,0:T(4,128)S(1)} %pad_maximum_fusion), channel_id=1, source_target_pairs={{8,0},{9,1},{10,2},{11,3},{12,4},{13,5},{14,6},{15,7},{1,8},{0,9},... | collective-permute-start | bytes 12296 | tf_op jit(solution)/shard_map/ppermute | solution.py:443
  15.8 6.3 %collective-permute-start.4 = (f32[4,256]{1,0:T(4,128)S(1)}, f32[4,256]{1,0:T(4,128)S(1)}, u32[]{:S(2)}, u32[]{:S(2)}) collective-permute-start(f32[4,256]{1,0:T(4,128)S(1)} %pad_maximum_fusion), channel_id=1, source_target_pairs={{4,0},{5,1},{6,2},{7,3},{8,4},{9,5},{10,6},{11,7},{12,8},{13,9},{1... | collective-permute-start | bytes 12296 | tf_op jit(solution)/shard_map/ppermute | solution.py:443
  18.3 0.9 copy-start.1
  19.3 0.9 copy-start.2
  20.2 0.9 copy-start.3
  21.1 1.0 copy-start
  22.1 0.7 copy-start.4
  116.5 2.4 %collective-permute-start.7 = (f32[528,256]{1,0:T(8,128)S(1)}, f32[528,256]{1,0:T(8,128)S(1)}, u32[]{:S(2)}, u32[]{:S(2)}) collective-permute-start(f32[528,256]{1,0:T(8,128)S(1)} %get-tuple-element.12.state_ref), channel_id=1, source_target_pairs={{0,1},{1,0},{2,3},{3,2},{4,5},{5,4},{6,7},{7,6},{8,9},{9,8},{10,11... | collective-permute-start | bytes 1622024 | tf_op jit(solution)/shard_map/ppermute | solution.py:491
  116.6 2.3 %collective-permute-start.8 = (f32[272,256]{1,0:T(8,128)S(1)}, f32[272,256]{1,0:T(8,128)S(1)}, u32[]{:S(2)}, u32[]{:S(2)}) collective-permute-start(f32[272,256]{1,0:T(8,128)S(1)} %get-tuple-element.13.info_ref), channel_id=1, source_target_pairs={{0,1},{1,0},{2,3},{3,2},{4,5},{5,4},{6,7},{7,6},{8,9},{9,8},{10,11... | collective-permute-start | bytes 835592 | tf_op jit(solution)/shard_map/ppermute | solution.py:492
  144.4 11.5 %collective-permute-start.10 = (f32[1,256,256]{2,1,0:T(8,128)S(1)}, f32[1,256,256]{2,1,0:T(8,128)S(1)}, u32[]{:S(2)}, u32[]{:S(2)}) collective-permute-start(f32[1,256,256]{2,1,0:T(8,128)S(1)} %get-tuple-element.15), channel_id=1, source_target_pairs={{0,0},{1,16},{2,2},{3,18},{4,4},{5,20},{6,6},{7,22},{8,8},{9,24},{... | collective-permute-start | bytes 786440 | tf_op jit(solution)/shard_map/ppermute | solution.py:506
  148.8 7.1 %collective-permute-start.9 = (f32[1,256]{1,0:T(1,128)S(1)}, f32[1,256]{1,0:T(1,128)S(1)}, u32[]{:S(2)}, u32[]{:S(2)}) collective-permute-start(f32[1,256]{1,0:T(1,128)S(1)} %get-tuple-element.14), channel_id=1, source_target_pairs={{0,0},{1,16},{2,2},{3,18},{4,4},{5,20},{6,6},{7,22},{8,8},{9,24},{... | collective-permute-start | bytes 3080 | tf_op jit(solution)/shard_map/ppermute | solution.py:506

commit v3 on v2

--- a/solution.py
+++ b/solution.py
@@ -13,26 +13,6 @@
 EXTRA = ROWS + ROWS // 2
 BOARD = ROWS * (EXTRA + ROWS)
 FAN = 4
-
-
-def dot_nn(left, right):
-    return lax.dot_general(
-        left,
-        right,
-        (((1,), (0,)), ((), ())),
-        precision=lax.Precision.HIGHEST,
-        preferred_element_type=jnp.float32,
-    )
-
-
-def dot_nt(left, right):
-    return lax.dot_general(
-        left,
-        right,
-        (((1,), (1,)), ((), ())),
-        precision=lax.Precision.HIGHEST,
-        preferred_element_type=jnp.float32,
-    )
 
 
 def pieces(x, count):
@@ -260,20 +240,33 @@
     return jnp.where(row == 0, values, 0.0)
 
 
-def maps_kernel(transition_ref, sensing_ref, noise_ref, left_ref, right_ref, consts_ref):
+def maps_kernel(
+    transition_ref,
+    sensing_ref,
+    noise_ref,
+    prior_ref,
+    left_ref,
+    right_ref,
+    fresh_ref,
+    sensed_noise_ref,
+    sensed_fresh_ref,
+):
     n = transition_ref.shape[0]
+    o = sensing_ref.shape[0]
     transition = transition_ref[...]
     sensing = sensing_ref[...]
     noise = noise_ref[...]
-    maps = jnp.concatenate([transition, dot_nn(sensing, transition)], axis=0)
+    sensed = exact_nn(sensing, transition)
+    maps = jnp.concatenate([transition, sensing, sensed], axis=0)
     high, low, least = pieces(maps, 3)
-    left_ref[...] = jnp.concatenate([high, low, least, high], axis=1)
     right_ref[...] = jnp.concatenate([high, high, low, least], axis=1)
-    noise_sensed = dot_nt(noise, sensing)
-    consts_ref[0:n, 0:n] = noise
-    consts_ref[0:n, n:] = noise_sensed
-    consts_ref[n:, 0:n] = jnp.zeros((sensing.shape[0], n), jnp.float32)
-    consts_ref[n:, n:] = dot_nn(sensing, noise_sensed)
+    left = jnp.concatenate([high, low, least, high], axis=1)
+    left_ref[0:n] = left[0:n]
+    left_ref[n:] = left[n + o :]
+    sensed_noise_ref[...] = exact_nn(sensing, exact_nt(noise, sensing))
+    carried = exact_nt(prior_ref[...], jnp.concatenate([transition, sensed], axis=0))
+    fresh_ref[...] = exact_nn(transition, carried[:, 0:n]) + noise
+    sensed_fresh_ref[...] = exact_nn(sensed, carried[:, n:])
 
 
 def window_kernel(
@@ -283,19 +276,23 @@
     rows_ref,
     left_ref,
     right_ref,
-    consts_ref,
+    noise_ref,
+    fresh_ref,
+    sensed_noise_ref,
+    sensed_fresh_ref,
     mean_ref,
-    prior_ref,
     state_ref,
     info_ref,
+    spread_ref,
+    before_ref,
     moved_ref,
     waiting_ref,
     inverse_ref,
     sensed_ref,
     board,
 ):
-    n = prior_ref.shape[0]
-    o = left_ref.shape[0] - n
+    n = noise_ref.shape[0]
+    o = sensed_noise_ref.shape[0]
     begin = begin_ref[0]
     eye_sense = unit(o)
 
@@ -305,62 +302,62 @@
     def line_at(k):
         return rows_ref[pl.ds(jnp.minimum(k, steps - 1), 1), :]
 
-    def first_spread(k, spread):
-        line = line_at(k)
-        return spread + consts_ref[n:, n:] + eye_sense * line[:, o:]
-
-    moved_ref[0:n] = jnp.zeros((n, n), jnp.float32)
-    moved_ref[n : 2 * n] = unit(n)
-    moved_ref[2 * n :] = jnp.zeros((VECTOR, n), jnp.float32)
+    def innovation(k, spread):
+        return spread + sensed_noise_ref[...] + eye_sense * line_at(k)[:, o:]
+
+    moved_ref[0:n] = unit(n)
+    moved_ref[n:] = jnp.zeros((VECTOR, n), jnp.float32)
     waiting_ref[...] = jnp.zeros_like(waiting_ref)
     inverse_ref[...] = jnp.zeros_like(inverse_ref)
     info_ref[...] = jnp.zeros_like(info_ref)
-
-    def through_sensed(spread):
-        half = join_nt(left_moving(spread), right_ref[n:])
-        return join_nn(left_ref[n:], right_moving(half))
-
-    sensed_ref[...] = first_spread(
-        0, jnp.where(begin == 0, through_sensed(prior_ref[...]), 0.0)
-    )
+    spread_ref[...] = jnp.where(begin == 0, fresh_ref[...], noise_ref[...])
+    sensed_ref[...] = innovation(0, jnp.where(begin == 0, sensed_fresh_ref[...], 0.0))
 
     def update():
         white = join_nt(waiting_ref[...], inverse_ref[...])
-        left = left_of(white)
-        info_ref[...] = info_ref[...] + join_nt(left[n:], right_of(white[n : 2 * n]))
-        return moved_ref[...] - join_nt(left, right_of(white[0:n]))
+        left = left_of(white[n:])
+        info_ref[...] = info_ref[...] + join_nt(left, right_of(white[n : 2 * n]))
+        return moved_ref[...] - join_nt(left, right_of(white[0:n])), white[0:n]
 
     def step(k, carry):
         ((_, inverse),) = factor_small([sensed_ref[...]], board)
         now = wrap(begin + k)
-        later = wrap(now + 1)
-        state = update()
-        state = jnp.where(
+        renewed = wrap(now + 1) == 0
+        spread = spread_ref[...]
+        seen = join_nt(left_moving(spread), right_ref[...])
+        ready = right_moving(seen)
+        ahead = join_nn(left_ref[0:n], ready[:, 0 : n + o])
+        sensed_ahead = join_nn(left_ref[n:], ready[:, n:])
+        move, _ = update()
+        move = jnp.where(
             now == 0,
-            jnp.concatenate(
-                [prior_ref[...], jnp.zeros((n, n), jnp.float32), first_of(mean_ref[...])], axis=0
-            ),
-            state,
+            jnp.concatenate([jnp.zeros((n, n), jnp.float32), first_of(mean_ref[...])], axis=0),
+            move,
         )
-        moved = join_nt(left_moving(state), right_ref[...])
-        ahead = join_nn(left_ref[0:n], right_moving(moved[0:n])) + consts_ref[0:n]
-        moved_ref[0:n] = ahead[:, 0:n]
-        moved_ref[n:] = moved[n:, 0:n]
-        waiting_ref[0:n] = left_of(ahead[:, n:])
-        waiting_ref[n : 2 * n] = left_of(moved[n : 2 * n, n:])
-        waiting_ref[2 * n :] = left_of(moved[2 * n :, n:] - first_of(line_at(k)[:, 0:o]))
-        kept = through_sensed(jnp.where(later == 0, prior_ref[...], ahead[:, 0:n]))
-        gained = exact_nt(join_nn(left_ref[n:], right_moving(ahead[:, n:])), inverse)
-        gained = jnp.where(later == 0, 0.0, gained)
-        sensed_ref[...] = first_spread(k + 1, kept - exact_nt(gained, gained))
-        inverse_ref[...] = right_of(inverse)
+        move = left_moving(move)
+        moved_ref[...] = join_nt(move, right_ref[0:n])
+        errors = join_nt(move, right_ref[n + o :])
+        waiting_ref[0:n] = left_of(seen[:, n : n + o])
+        waiting_ref[n : 2 * n] = left_of(errors[0:n])
+        waiting_ref[2 * n :] = left_of(errors[n:] - first_of(line_at(k)[:, 0:o]))
+        before_ref[...] = spread
+        gained = exact_nt(sensed_ahead[:, 0:o], inverse)
+        sensed_ref[...] = innovation(
+            k + 1,
+            jnp.where(renewed, sensed_fresh_ref[...], sensed_ahead[:, o:] - exact_nt(gained, gained)),
+        )
+        inverse_right = right_of(inverse)
+        inverse_ref[...] = inverse_right
+        gain = join_nt(left_of(ahead[:, n:]), inverse_right)
+        later = ahead[:, 0:n] + noise_ref[...] - join_nt(left_of(gain), right_of(gain))
+        spread_ref[...] = jnp.where(renewed, fresh_ref[...], later)
         return carry
 
     lax.fori_loop(0, steps, step, 0)
-    state = update()
-    ((root, _),) = factor([state[0:n]], board)
+    move, gain = update()
+    ((root, _),) = factor([before_ref[...] - near_nt(gain, gain)], board)
     state_ref[0:n] = root
-    state_ref[n:] = state[n:]
+    state_ref[n:] = move
 
 
 def meet_kernel(
@@ -465,28 +462,45 @@
     def shape(*dims):
         return jax.ShapeDtypeStruct(dims, jnp.float32)
 
-    passes = jax.ShapeDtypeStruct((n + o, 4 * n), jnp.bfloat16)
-    left, right, consts = pl.pallas_call(
+    left, right, fresh, sensed_noise, sensed_fresh = pl.pallas_call(
         maps_kernel,
-        out_shape=(passes, passes, shape(n + o, n + o)),
-        in_specs=[vmem] * 3,
-        out_specs=(vmem, vmem, vmem),
+        out_shape=(
+            jax.ShapeDtypeStruct((n + o, 4 * n), jnp.bfloat16),
+            jax.ShapeDtypeStruct((n + 2 * o, 4 * n), jnp.bfloat16),
+            shape(n, n),
+            shape(o, o),
+            shape(o, o),
+        ),
+        in_specs=[vmem] * 4,
+        out_specs=(vmem,) * 5,
         compiler_params=params,
-    )(transition, sensing, process_noise)
+    )(transition, sensing, process_noise, prior_covariance)
     state, info = pl.pallas_call(
         functools.partial(window_kernel, half, devices),
         out_shape=(shape(2 * n + VECTOR, n), shape(n + VECTOR, n)),
-        in_specs=[smem] + [vmem] * 6,
+        in_specs=[smem] + [vmem] * 8,
         out_specs=(vmem, vmem),
         scratch_shapes=[
-            pltpu.VMEM((2 * n + VECTOR, n), jnp.float32),
+            pltpu.VMEM((n, n), jnp.float32),
+            pltpu.VMEM((n, n), jnp.float32),
+            pltpu.VMEM((n + VECTOR, n), jnp.float32),
             pltpu.VMEM((2 * n + VECTOR, 3 * o), jnp.bfloat16),
             pltpu.VMEM((o, 3 * o), jnp.bfloat16),
             pltpu.VMEM((o, o), jnp.float32),
             pltpu.VMEM((1, 2, BOARD, o), jnp.float32),
         ],
         compiler_params=params,
-    )(begin.reshape(1), rows, left, right, consts, prior_mean.reshape(1, n), prior_covariance)
+    )(
+        begin.reshape(1),
+        rows,
+        left,
+        right,
+        process_noise,
+        fresh,
+        sensed_noise,
+        sensed_fresh,
+        prior_mean.reshape(1, n),
+    )
     swap = [(i, i ^ 1) for i in range(devices)]
     far_state = lax.ppermute(state, "tm", swap)
     far_info = lax.ppermute(info, "tm", swap)

time: 157 us -> 162 us (1.032)
  Pallas kernels: 120 us -> 123 us
    pallas_call x1, Pallas kernels: 93.7 us -> 96.2 us  [shards(): pl.pallas_call(functools.partial(window_kernel, half, devices), out_shape...]
    unnamed x15 -> x17, local copies, waits for them, and re-layouts: 5.41 us -> 6.36 us
where the time goes in v3:
time: 162 us; the launch traced here: 161 us
  Pallas kernels  123 us (76%)
  starting transfers between devices  23.9 us (15%)
  waiting for transfers between devices  6.87 us (4%)
  local copies, waits for them, and re-layouts  6.41 us (4%)
    pallas_call x1, Pallas kernels, shards(): pl.pallas_call(functools.partial(window_kernel, half, devices), out_shape...  96.2 us
    pallas_call x1, Pallas kernels, shards(): pl.pallas_call(meet_kernel, out_shape=(shape(1, n), shape(1, n, n)), in_s...  25.4 us
    ppermute x4, starting transfers between devices, gather_rows(): lax.ppermute(rows, axis, [((begins[i] + j) % devices, i) for i in range(d...  8.93 us
    ppermute x3, starting transfers between devices, gather_rows(): parts.append(lax.ppermute(rows[:size], axis, pairs))  7.98 us
    ppermute x2, starting transfers between devices, shards(): return (lax.ppermute(mean, 'tm', home), lax.ppermute(cov, 'tm', home))  6.46 us
    unnamed x17, local copies, waits for them, and re-layouts  6.36 us
    ppermute x2, waiting for transfers between devices, shards(): return (lax.ppermute(mean, 'tm', home), lax.ppermute(cov, 'tm', home))  4.98 us
  transfers between devices with their start and end apart: 11, of which 2 were waited for; matrix products, arithmetic and copies ran while one was open for 0% of the time, Pallas kernels for 1%

profile of v3, /device:TPU:1, one launch (start us, length us, event | category | flops | bytes accessed | tf_op | source)
XLA Modules:
  0.0 161.3 jit_solution(10873745399386586802)
XLA Ops:
  0.6 0.0 copy-start.6
  0.6 0.7 constant_dynamic-update-slice_fusion.1
  1.3 0.0 copy-done.6
  1.3 5.7 %collective-permute-start.3 = (f32[1,256]{1,0:T(1,128)S(1)}, f32[1,256]{1,0:T(1,128)S(1)}, u32[]{:S(2)}, u32[]{:S(2)}) collective-permute-start(f32[1,256]{1,0:T(1,128)S(1)} %constant_dynamic-update-slice_fusion), channel_id=1, source_target_pairs={{20,0},{4,1},{22,2},{6,3},{24,4},{8,5},{26,6},{10,7},{28,8},{12,9}... | collective-permute-start | bytes 3080 | tf_op jit(solution)/shard_map/ppermute | solution.py:430
  7.0 0.0 collective-permute-start.2
  7.0 2.6 %collective-permute-start.1 = (f32[1,256]{1,0:T(1,128)S(1)}, f32[1,256]{1,0:T(1,128)S(1)}, u32[]{:S(2)}, u32[]{:S(2)}) collective-permute-start(f32[1,256]{1,0:T(1,128)S(1)} %constant_dynamic-update-slice_fusion), channel_id=1, source_target_pairs={{18,0},{2,1},{20,2},{4,3},{22,4},{6,5},{24,6},{8,7},{26,8},{10,9},... | collective-permute-start | bytes 3080 | tf_op jit(solution)/shard_map/ppermute | solution.py:430
  9.6 0.6 collective-permute-start
  10.3 0.0 collective-permute-done.3
  10.3 0.0 collective-permute-done.2
  10.3 0.0 collective-permute-done.1
  10.3 0.0 collective-permute-done
  10.3 5.4 %collective-permute-start.6 = (f32[4,256]{1,0:T(4,128)S(1)}, f32[4,256]{1,0:T(4,128)S(1)}, u32[]{:S(2)}, u32[]{:S(2)}) collective-permute-start(f32[4,256]{1,0:T(4,128)S(1)} %pad_maximum_fusion), channel_id=1, source_target_pairs={{12,0},{13,1},{14,2},{15,3},{1,4},{0,5},{3,6},{2,7},{5,8},{4,9},{7... | collective-permute-start | bytes 12296 | tf_op jit(solution)/shard_map/ppermute | solution.py:440
  15.8 0.0 collective-permute-start.5
  15.8 2.6 %collective-permute-start.4 = (f32[4,256]{1,0:T(4,128)S(1)}, f32[4,256]{1,0:T(4,128)S(1)}, u32[]{:S(2)}, u32[]{:S(2)}) collective-permute-start(f32[4,256]{1,0:T(4,128)S(1)} %pad_maximum_fusion), channel_id=1, source_target_pairs={{4,0},{5,1},{6,2},{7,3},{8,4},{9,5},{10,6},{11,7},{12,8},{13,9},{1... | collective-permute-start | bytes 12296 | tf_op jit(solution)/shard_map/ppermute | solution.py:440
  18.3 0.0 copy-start
  18.3 0.9 copy-done
  19.3 0.0 copy-start.2
  19.3 0.9 copy-done.2
  20.2 0.0 copy-start.3
  20.2 0.9 copy-done.3
  21.2 0.0 copy-start.4
  21.2 0.9 copy-done.4
  22.1 0.0 copy-start.1
  22.1 1.7 %shard_map.86 = (bf16[384,1024]{1,0:T(8,128)(2,1)S(1)}, bf16[512,1024]{1,0:T(8,128)(2,1)S(1)}, f32[256,256]{1,0:T(8,128)S(1)}, f32[128,128]{1,0:T(8,128)S(1)}, f32[128,128]{1,0:T(8,128)S(1)}) custom-call(f32[256,256]{1,0:T(8,128)S(1)} %copy-done.2, f32[128,256]{1,0:T(8,128)S(1)} %copy-done.4, f32[256,256]{1,0:T(8,128)S(1)} %copy-done, f32[256,256]{1,0:T(8,128)S(1)} %copy-done.3), custom_call_target="tpu_custom_call" | custom-call | tf_op jit(solution)/shard_map/pallas_call | solution.py:465
  23.8 0.0 collective-permute-done.6
  23.8 0.0 collective-permute-done.5
  23.8 0.0 collective-permute-done.4
  23.9 0.0 copy-start.5
  23.9 0.0 copy-done.1
  23.9 0.7 copy-done.5
  24.6 96.2 %shard_map.87 = (f32[528,256]{1,0:T(8,128)S(1)}, f32[272,256]{1,0:T(8,128)S(1)}) custom-call(s32[1]{0:T(128)} %bitcast.1.begin_ref, f32[16,256]{1,0:T(8,128)S(1)} %concatenate.12.rows_ref, bf16[384,1024]{1,0:T(8,128)(2,1)S(1)} %get-tuple-element.11.left_ref, bf16[512,1024]{1,0:T(8,128)(2,1)S(1)} %get-tuple-element.12.right_ref, f32[256,256]{1,0:T(8,128)S(1)} %copy-done.1, ...), custom_call_target="tpu_custom_call" | custom-call | tf_op jit(solution)/shard_map/pallas_call | solution.py:478
  120.8 0.1 collective-permute-start.7
  120.9 0.5 collective-permute-start.8
  121.4 1.8 %collective-permute-done.8.far_info_ref = f32[272,256]{1,0:T(8,128)S(1)} collective-permute-done((f32[272,256]{1,0:T(8,128)S(1)}, f32[272,256]{1,0:T(8,128)S(1)}, u32[]{:S(2)}, u32[]{:S(2)}) %collective-permute-start.8) | collective-permute-done | bytes 278560 | tf_op jit(solution)/shard_map/ppermute | solution.py:506
  123.2 0.0 collective-permute-done.7.far_state_ref
  123.2 25.4 %shard_map.88 = (f32[1,256]{1,0:T(1,128)S(1)}, f32[1,256,256]{2,1,0:T(8,128)S(1)}) custom-call(s32[1]{0:T(128)} %bitcast.role_ref, f32[528,256]{1,0:T(8,128)S(1)} %get-tuple-element.16.state_ref, f32[272,256]{1,0:T(8,128)S(1)} %get-tuple-element.17.info_ref, f32[528,256]{1,0:T(8,128)S(1)} %collective-permute-done.7.far_state_ref, ...), custom_call_target="tpu_custom_call" | custom-call | tf_op jit(solution)/shard_map/pallas_call | solution.py:507
  148.6 4.4 %collective-permute-start.10 = (f32[1,256,256]{2,1,0:T(8,128)S(1)}, f32[1,256,256]{2,1,0:T(8,128)S(1)}, u32[]{:S(2)}, u32[]{:S(2)}) collective-permute-start(f32[1,256,256]{2,1,0:T(8,128)S(1)} %get-tuple-element.19), channel_id=1, source_target_pairs={{0,0},{1,16},{2,2},{3,18},{4,4},{5,20},{6,6},{7,22},{8,8},{9,24},{... | collective-permute-start | bytes 786440 | tf_op jit(solution)/shard_map/ppermute | solution.py:520
  153.0 2.1 %collective-permute-start.9 = (f32[1,256]{1,0:T(1,128)S(1)}, f32[1,256]{1,0:T(1,128)S(1)}, u32[]{:S(2)}, u32[]{:S(2)}) collective-permute-start(f32[1,256]{1,0:T(1,128)S(1)} %get-tuple-element.18), channel_id=1, source_target_pairs={{0,0},{1,16},{2,2},{3,18},{4,4},{5,20},{6,6},{7,22},{8,8},{9,24},{... | collective-permute-start | bytes 3080 | tf_op jit(solution)/shard_map/ppermute | solution.py:520
  155.1 5.0 %collective-permute-done.9 = f32[1,256]{1,0:T(1,128)S(1)} collective-permute-done((f32[1,256]{1,0:T(1,128)S(1)}, f32[1,256]{1,0:T(1,128)S(1)}, u32[]{:S(2)}, u32[]{:S(2)}) %collective-permute-start.9) | collective-permute-done | bytes 1056 | tf_op jit(solution)/shard_map/ppermute | solution.py:520
  160.1 0.0 collective-permute-done.10
  160.1 0.6 copy.12
  160.6 0.7 copy.13
  (3 shorter events, 0.1 us)
Async XLA Ops:
  0.6 0.7 copy-start.6
  1.3 8.9 %collective-permute-start.3 = (f32[1,256]{1,0:T(1,128)S(1)}, f32[1,256]{1,0:T(1,128)S(1)}, u32[]{:S(2)}, u32[]{:S(2)}) collective-permute-start(f32[1,256]{1,0:T(1,128)S(1)} %constant_dynamic-update-slice_fusion), channel_id=1, source_target_pairs={{20,0},{4,1},{22,2},{6,3},{24,4},{8,5},{26,6},{10,7},{28,8},{12,9}... | collective-permute-start | bytes 3080 | tf_op jit(solution)/shard_map/ppermute | solution.py:430
  7.0 3.3 %collective-permute-start.2 = (f32[1,256]{1,0:T(1,128)S(1)}, f32[1,256]{1,0:T(1,128)S(1)}, u32[]{:S(2)}, u32[]{:S(2)}) collective-permute-start(f32[1,256]{1,0:T(1,128)S(1)} %constant_dynamic-update-slice_fusion), channel_id=1, source_target_pairs={{19,0},{3,1},{21,2},{5,3},{23,4},{7,5},{25,6},{9,7},{27,8},{11,9},... | collective-permute-start | bytes 3080 | tf_op jit(solution)/shard_map/ppermute | solution.py:430
  7.0 3.3 %collective-permute-start.1 = (f32[1,256]{1,0:T(1,128)S(1)}, f32[1,256]{1,0:T(1,128)S(1)}, u32[]{:S(2)}, u32[]{:S(2)}) collective-permute-start(f32[1,256]{1,0:T(1,128)S(1)} %constant_dynamic-update-slice_fusion), channel_id=1, source_target_pairs={{18,0},{2,1},{20,2},{4,3},{22,4},{6,5},{24,6},{8,7},{26,8},{10,9},... | collective-permute-start | bytes 3080 | tf_op jit(solution)/shard_map/ppermute | solution.py:430
  9.6 0.7 collective-permute-start
  10.3 13.5 %collective-permute-start.6 = (f32[4,256]{1,0:T(4,128)S(1)}, f32[4,256]{1,0:T(4,128)S(1)}, u32[]{:S(2)}, u32[]{:S(2)}) collective-permute-start(f32[4,256]{1,0:T(4,128)S(1)} %pad_maximum_fusion), channel_id=1, source_target_pairs={{12,0},{13,1},{14,2},{15,3},{1,4},{0,5},{3,6},{2,7},{5,8},{4,9},{7... | collective-permute-start | bytes 12296 | tf_op jit(solution)/shard_map/ppermute | solution.py:440
  15.8 8.1 %collective-permute-start.5 = (f32[4,256]{1,0:T(4,128)S(1)}, f32[4,256]{1,0:T(4,128)S(1)}, u32[]{:S(2)}, u32[]{:S(2)}) collective-permute-start(f32[4,256]{1,0:T(4,128)S(1)} %pad_maximum_fusion), channel_id=1, source_target_pairs={{8,0},{9,1},{10,2},{11,3},{12,4},{13,5},{14,6},{15,7},{1,8},{0,9},... | collective-permute-start | bytes 12296 | tf_op jit(solution)/shard_map/ppermute | solution.py:440
  15.8 8.1 %collective-permute-start.4 = (f32[4,256]{1,0:T(4,128)S(1)}, f32[4,256]{1,0:T(4,128)S(1)}, u32[]{:S(2)}, u32[]{:S(2)}) collective-permute-start(f32[4,256]{1,0:T(4,128)S(1)} %pad_maximum_fusion), channel_id=1, source_target_pairs={{4,0},{5,1},{6,2},{7,3},{8,4},{9,5},{10,6},{11,7},{12,8},{13,9},{1... | collective-permute-start | bytes 12296 | tf_op jit(solution)/shard_map/ppermute | solution.py:440
  18.3 0.9 copy-start
  19.3 0.9 copy-start.2
  20.2 0.9 copy-start.3
  21.2 0.9 copy-start.4
  22.1 1.8 %copy-start.1 = (f32[256,256]{1,0:T(8,128)S(1)}, f32[256,256]{1,0:T(8,128)}, u32[]{:S(2)}) copy-start(f32[256,256]{1,0:T(8,128)} %noise_ref.3) | copy-start | bytes 786436
  23.9 0.7 copy-start.5
  120.8 2.4 %collective-permute-start.7 = (f32[528,256]{1,0:T(8,128)S(1)}, f32[528,256]{1,0:T(8,128)S(1)}, u32[]{:S(2)}, u32[]{:S(2)}) collective-permute-start(f32[528,256]{1,0:T(8,128)S(1)} %get-tuple-element.16.state_ref), channel_id=1, source_target_pairs={{0,1},{1,0},{2,3},{3,2},{4,5},{5,4},{6,7},{7,6},{8,9},{9,8},{10,11... | collective-permute-start | bytes 1622024 | tf_op jit(solution)/shard_map/ppermute | solution.py:505
  120.9 2.3 %collective-permute-start.8 = (f32[272,256]{1,0:T(8,128)S(1)}, f32[272,256]{1,0:T(8,128)S(1)}, u32[]{:S(2)}, u32[]{:S(2)}) collective-permute-start(f32[272,256]{1,0:T(8,128)S(1)} %get-tuple-element.17.info_ref), channel_id=1, source_target_pairs={{0,1},{1,0},{2,3},{3,2},{4,5},{5,4},{6,7},{7,6},{8,9},{9,8},{10,11... | collective-permute-start | bytes 835592 | tf_op jit(solution)/shard_map/ppermute | solution.py:506
  148.6 11.5 %collective-permute-start.10 = (f32[1,256,256]{2,1,0:T(8,128)S(1)}, f32[1,256,256]{2,1,0:T(8,128)S(1)}, u32[]{:S(2)}, u32[]{:S(2)}) collective-permute-start(f32[1,256,256]{2,1,0:T(8,128)S(1)} %get-tuple-element.19), channel_id=1, source_target_pairs={{0,0},{1,16},{2,2},{3,18},{4,4},{5,20},{6,6},{7,22},{8,8},{9,24},{... | collective-permute-start | bytes 786440 | tf_op jit(solution)/shard_map/ppermute | solution.py:520
  153.0 7.1 %collective-permute-start.9 = (f32[1,256]{1,0:T(1,128)S(1)}, f32[1,256]{1,0:T(1,128)S(1)}, u32[]{:S(2)}, u32[]{:S(2)}) collective-permute-start(f32[1,256]{1,0:T(1,128)S(1)} %get-tuple-element.18), channel_id=1, source_target_pairs={{0,0},{1,16},{2,2},{3,18},{4,4},{5,20},{6,6},{7,22},{8,8},{9,24},{... | collective-permute-start | bytes 3080 | tf_op jit(solution)/shard_map/ppermute | solution.py:520

commit v4 on v3

--- a/solution.py
+++ b/solution.py
@@ -84,7 +84,9 @@
     return join_nt(left_of(left), right_of(right))
 
 
-def factor_small(matrices, board):
+def factor_small(matrices, board, beside=()):
+    beside = list(beside)
+    done = 0
     side = matrices[0].shape[0]
     count = side // ROWS
     shape = (ROWS, side)
@@ -114,6 +116,9 @@
             pivots = jnp.ones(shape, jnp.float32)
             for i in range(0, ROWS, 2):
                 p = base + i
+                while done < len(beside) and done * side <= p * len(beside):
+                    beside[done]()
+                    done += 1
                 pair = (lane == p) | (lane == p + 1)
                 a, b, c = block[i, i], block[i + 1, i], block[i + 1, i + 1]
                 det = a * c - b * b
@@ -320,32 +325,73 @@
         return moved_ref[...] - join_nt(left, right_of(white[0:n])), white[0:n]
 
     def step(k, carry):
-        ((_, inverse),) = factor_small([sensed_ref[...]], board)
         now = wrap(begin + k)
         renewed = wrap(now + 1) == 0
-        spread = spread_ref[...]
-        seen = join_nt(left_moving(spread), right_ref[...])
-        ready = right_moving(seen)
-        ahead = join_nn(left_ref[0:n], ready[:, 0 : n + o])
-        sensed_ahead = join_nn(left_ref[n:], ready[:, n:])
-        move, _ = update()
-        move = jnp.where(
-            now == 0,
-            jnp.concatenate([jnp.zeros((n, n), jnp.float32), first_of(mean_ref[...])], axis=0),
-            move,
-        )
-        move = left_moving(move)
-        moved_ref[...] = join_nt(move, right_ref[0:n])
-        errors = join_nt(move, right_ref[n + o :])
-        waiting_ref[0:n] = left_of(seen[:, n : n + o])
-        waiting_ref[n : 2 * n] = left_of(errors[0:n])
-        waiting_ref[2 * n :] = left_of(errors[n:] - first_of(line_at(k)[:, 0:o]))
-        before_ref[...] = spread
-        gained = exact_nt(sensed_ahead[:, 0:o], inverse)
-        sensed_ref[...] = innovation(
-            k + 1,
-            jnp.where(renewed, sensed_fresh_ref[...], sensed_ahead[:, o:] - exact_nt(gained, gained)),
-        )
+        cuts = [(lo, min(n, lo + LANES)) for lo in range(0, n, LANES)]
+        tall = [(lo, hi + (VECTOR if hi == n else 0)) for lo, hi in cuts]
+        held = {}
+
+        def see(lo, hi):
+            held["seen", lo] = join_nt(left_moving(spread_ref[lo:hi]), right_ref[...])
+
+        def prepare():
+            held["seen"] = jnp.concatenate([held["seen", lo] for lo, _ in cuts], axis=0)
+            held["ready"] = right_moving(held["seen"])
+
+        def look_ahead(lo, hi):
+            held["ahead", lo] = join_nn(left_ref[lo:hi], held["ready"][:, 0 : n + o])
+
+        def sense_ahead():
+            held["sensed"] = join_nn(left_ref[n:], held["ready"][:, n:])
+
+        def whiten_gain():
+            gain = join_nt(waiting_ref[0:n], inverse_ref[...])
+            held["gain"] = right_of(gain)
+
+        def whiten_move():
+            white = join_nt(waiting_ref[n:], inverse_ref[...])
+            held["left"] = left_of(white)
+            held["right"] = right_of(white[0:n])
+
+        def inform(lo, hi):
+            change = join_nt(held["left"][lo:hi], held["right"])
+            info_ref[lo:hi] = info_ref[lo:hi] + change
+
+        def correct(lo, hi):
+            move = moved_ref[lo:hi] - join_nt(held["left"][lo:hi], held["gain"])
+            start = jnp.zeros((min(hi, n) - lo, n), jnp.float32)
+            if hi > n:
+                start = jnp.concatenate([start, first_of(mean_ref[...])], axis=0)
+            held["move", lo] = left_moving(jnp.where(now == 0, start, move))
+
+        def advance(lo, hi):
+            moved_ref[lo:hi] = join_nt(held["move", lo], right_ref[0:n])
+
+        def err(lo, hi):
+            errors = join_nt(held["move", lo], right_ref[n + o :])
+            if hi > n:
+                line = first_of(line_at(k)[:, 0:o])
+                errors = jnp.concatenate([errors[: n - lo], errors[n - lo :] - line], axis=0)
+            waiting_ref[n + lo : n + hi] = left_of(errors)
+
+        def keep():
+            waiting_ref[0:n] = left_of(held["seen"][:, n : n + o])
+            before_ref[...] = spread_ref[...]
+
+        beside = [functools.partial(see, *cut) for cut in cuts]
+        beside += [whiten_gain, prepare, whiten_move]
+        beside += [functools.partial(look_ahead, *cut) for cut in cuts]
+        beside += [sense_ahead]
+        beside += [functools.partial(correct, *cut) for cut in tall]
+        beside += [functools.partial(inform, *cut) for cut in tall]
+        beside += [functools.partial(advance, *cut) for cut in tall]
+        beside += [functools.partial(err, *cut) for cut in tall]
+        beside += [keep]
+        ((_, inverse),) = factor_small([sensed_ref[...]], board, beside)
+        ahead = jnp.concatenate([held["ahead", lo] for lo, _ in cuts], axis=0)
+        gained = exact_nt(held["sensed"][:, 0:o], inverse)
+        sensed = held["sensed"][:, o:] - exact_nt(gained, gained)
+        sensed_ref[...] = innovation(k + 1, jnp.where(renewed, sensed_fresh_ref[...], sensed))
         inverse_right = right_of(inverse)
         inverse_ref[...] = inverse_right
         gain = join_nt(left_of(ahead[:, n:]), inverse_right)

time: 162 us -> 162 us (level)
  no operation moved by 1% of the time
where the time goes in v4:
time: 162 us; the launch traced here: 161 us
  Pallas kernels  123 us (76%)
  starting transfers between devices  23.9 us (15%)
  waiting for transfers between devices  6.87 us (4%)
  local copies, waits for them, and re-layouts  6.41 us (4%)
    pallas_call x1, Pallas kernels, shards(): pl.pallas_call(functools.partial(window_kernel, half, devices), out_shape...  96.3 us
    pallas_call x1, Pallas kernels, shards(): pl.pallas_call(meet_kernel, out_shape=(shape(1, n), shape(1, n, n)), in_s...  25.4 us
    ppermute x4, starting transfers between devices, gather_rows(): lax.ppermute(rows, axis, [((begins[i] + j) % devices, i) for i in range(d...  8.93 us
    ppermute x3, starting transfers between devices, gather_rows(): parts.append(lax.ppermute(rows[:size], axis, pairs))  7.98 us
    ppermute x2, starting transfers between devices, shards(): return (lax.ppermute(mean, 'tm', home), lax.ppermute(cov, 'tm', home))  6.46 us
    unnamed x17, local copies, waits for them, and re-layouts  6.36 us
    ppermute x2, waiting for transfers between devices, shards(): return (lax.ppermute(mean, 'tm', home), lax.ppermute(cov, 'tm', home))  4.98 us
  transfers between devices with their start and end apart: 11, of which 2 were waited for; matrix products, arithmetic and copies ran while one was open for 0% of the time, Pallas kernels for 1%

profile of v4, /device:TPU:1, one launch (start us, length us, event | category | flops | bytes accessed | tf_op | source)
XLA Modules:
  0.0 161.5 jit_solution(84506711984554498)
XLA Ops:
  0.6 0.0 copy-start.6
  0.6 0.7 constant_dynamic-update-slice_fusion.1
  1.3 0.0 copy-done.6
  1.3 5.7 %collective-permute-start.3 = (f32[1,256]{1,0:T(1,128)S(1)}, f32[1,256]{1,0:T(1,128)S(1)}, u32[]{:S(2)}, u32[]{:S(2)}) collective-permute-start(f32[1,256]{1,0:T(1,128)S(1)} %constant_dynamic-update-slice_fusion), channel_id=1, source_target_pairs={{20,0},{4,1},{22,2},{6,3},{24,4},{8,5},{26,6},{10,7},{28,8},{12,9}... | collective-permute-start | bytes 3080 | tf_op jit(solution)/shard_map/ppermute | solution.py:476
  7.0 0.0 collective-permute-start.2
  7.0 2.6 %collective-permute-start.1 = (f32[1,256]{1,0:T(1,128)S(1)}, f32[1,256]{1,0:T(1,128)S(1)}, u32[]{:S(2)}, u32[]{:S(2)}) collective-permute-start(f32[1,256]{1,0:T(1,128)S(1)} %constant_dynamic-update-slice_fusion), channel_id=1, source_target_pairs={{18,0},{2,1},{20,2},{4,3},{22,4},{6,5},{24,6},{8,7},{26,8},{10,9},... | collective-permute-start | bytes 3080 | tf_op jit(solution)/shard_map/ppermute | solution.py:476
  9.6 0.6 collective-permute-start
  10.3 0.0 collective-permute-done.3
  10.3 0.0 collective-permute-done.2
  10.3 0.0 collective-permute-done.1
  10.3 0.0 collective-permute-done
  10.3 5.4 %collective-permute-start.6 = (f32[4,256]{1,0:T(4,128)S(1)}, f32[4,256]{1,0:T(4,128)S(1)}, u32[]{:S(2)}, u32[]{:S(2)}) collective-permute-start(f32[4,256]{1,0:T(4,128)S(1)} %pad_maximum_fusion), channel_id=1, source_target_pairs={{12,0},{13,1},{14,2},{15,3},{1,4},{0,5},{3,6},{2,7},{5,8},{4,9},{7... | collective-permute-start | bytes 12296 | tf_op jit(solution)/shard_map/ppermute | solution.py:486
  15.8 0.0 collective-permute-start.5
  15.8 2.6 %collective-permute-start.4 = (f32[4,256]{1,0:T(4,128)S(1)}, f32[4,256]{1,0:T(4,128)S(1)}, u32[]{:S(2)}, u32[]{:S(2)}) collective-permute-start(f32[4,256]{1,0:T(4,128)S(1)} %pad_maximum_fusion), channel_id=1, source_target_pairs={{4,0},{5,1},{6,2},{7,3},{8,4},{9,5},{10,6},{11,7},{12,8},{13,9},{1... | collective-permute-start | bytes 12296 | tf_op jit(solution)/shard_map/ppermute | solution.py:486
  18.3 0.0 copy-start
  18.3 0.9 copy-done
  19.3 0.0 copy-start.2
  19.3 0.9 copy-done.2
  20.2 0.0 copy-start.3
  20.2 0.9 copy-done.3
  21.2 0.0 copy-start.4
  21.2 0.9 copy-done.4
  22.1 0.0 copy-start.1
  22.1 1.7 %shard_map.86 = (bf16[384,1024]{1,0:T(8,128)(2,1)S(1)}, bf16[512,1024]{1,0:T(8,128)(2,1)S(1)}, f32[256,256]{1,0:T(8,128)S(1)}, f32[128,128]{1,0:T(8,128)S(1)}, f32[128,128]{1,0:T(8,128)S(1)}) custom-call(f32[256,256]{1,0:T(8,128)S(1)} %copy-done.2, f32[128,256]{1,0:T(8,128)S(1)} %copy-done.4, f32[256,256]{1,0:T(8,128)S(1)} %copy-done, f32[256,256]{1,0:T(8,128)S(1)} %copy-done.3), custom_call_target="tpu_custom_call" | custom-call | tf_op jit(solution)/shard_map/pallas_call | solution.py:511
  23.8 0.0 collective-permute-done.6
  23.8 0.0 collective-permute-done.5
  23.8 0.0 collective-permute-done.4
  23.9 0.0 copy-start.5
  23.9 0.0 copy-done.1
  23.9 0.7 copy-done.5
  24.6 96.3 %shard_map.87 = (f32[528,256]{1,0:T(8,128)S(1)}, f32[272,256]{1,0:T(8,128)S(1)}) custom-call(s32[1]{0:T(128)} %bitcast.1.begin_ref, f32[16,256]{1,0:T(8,128)S(1)} %concatenate.12.rows_ref, bf16[384,1024]{1,0:T(8,128)(2,1)S(1)} %get-tuple-element.11.left_ref, bf16[512,1024]{1,0:T(8,128)(2,1)S(1)} %get-tuple-element.12.right_ref, f32[256,256]{1,0:T(8,128)S(1)} %copy-done.1, ...), custom_call_target="tpu_custom_call" | custom-call | tf_op jit(solution)/shard_map/pallas_call | solution.py:524
  120.9 0.1 collective-permute-start.7
  121.0 0.5 collective-permute-start.8
  121.5 1.8 %collective-permute-done.8.far_info_ref = f32[272,256]{1,0:T(8,128)S(1)} collective-permute-done((f32[272,256]{1,0:T(8,128)S(1)}, f32[272,256]{1,0:T(8,128)S(1)}, u32[]{:S(2)}, u32[]{:S(2)}) %collective-permute-start.8) | collective-permute-done | bytes 278560 | tf_op jit(solution)/shard_map/ppermute | solution.py:552
  123.3 0.0 collective-permute-done.7.far_state_ref
  123.3 25.4 %shard_map.88 = (f32[1,256]{1,0:T(1,128)S(1)}, f32[1,256,256]{2,1,0:T(8,128)S(1)}) custom-call(s32[1]{0:T(128)} %bitcast.role_ref, f32[528,256]{1,0:T(8,128)S(1)} %get-tuple-element.16.state_ref, f32[272,256]{1,0:T(8,128)S(1)} %get-tuple-element.17.info_ref, f32[528,256]{1,0:T(8,128)S(1)} %collective-permute-done.7.far_state_ref, ...), custom_call_target="tpu_custom_call" | custom-call | tf_op jit(solution)/shard_map/pallas_call | solution.py:553
  148.7 4.4 %collective-permute-start.10 = (f32[1,256,256]{2,1,0:T(8,128)S(1)}, f32[1,256,256]{2,1,0:T(8,128)S(1)}, u32[]{:S(2)}, u32[]{:S(2)}) collective-permute-start(f32[1,256,256]{2,1,0:T(8,128)S(1)} %get-tuple-element.19), channel_id=1, source_target_pairs={{0,0},{1,16},{2,2},{3,18},{4,4},{5,20},{6,6},{7,22},{8,8},{9,24},{... | collective-permute-start | bytes 786440 | tf_op jit(solution)/shard_map/ppermute | solution.py:566
  153.2 2.1 %collective-permute-start.9 = (f32[1,256]{1,0:T(1,128)S(1)}, f32[1,256]{1,0:T(1,128)S(1)}, u32[]{:S(2)}, u32[]{:S(2)}) collective-permute-start(f32[1,256]{1,0:T(1,128)S(1)} %get-tuple-element.18), channel_id=1, source_target_pairs={{0,0},{1,16},{2,2},{3,18},{4,4},{5,20},{6,6},{7,22},{8,8},{9,24},{... | collective-permute-start | bytes 3080 | tf_op jit(solution)/shard_map/ppermute | solution.py:566
  155.2 5.0 %collective-permute-done.9 = f32[1,256]{1,0:T(1,128)S(1)} collective-permute-done((f32[1,256]{1,0:T(1,128)S(1)}, f32[1,256]{1,0:T(1,128)S(1)}, u32[]{:S(2)}, u32[]{:S(2)}) %collective-permute-start.9) | collective-permute-done | bytes 1056 | tf_op jit(solution)/shard_map/ppermute | solution.py:566
  160.2 0.0 collective-permute-done.10
  160.2 0.6 copy.12
  160.8 0.7 copy.13
  (3 shorter events, 0.1 us)
Async XLA Ops:
  0.6 0.7 copy-start.6
  1.3 8.9 %collective-permute-start.3 = (f32[1,256]{1,0:T(1,128)S(1)}, f32[1,256]{1,0:T(1,128)S(1)}, u32[]{:S(2)}, u32[]{:S(2)}) collective-permute-start(f32[1,256]{1,0:T(1,128)S(1)} %constant_dynamic-update-slice_fusion), channel_id=1, source_target_pairs={{20,0},{4,1},{22,2},{6,3},{24,4},{8,5},{26,6},{10,7},{28,8},{12,9}... | collective-permute-start | bytes 3080 | tf_op jit(solution)/shard_map/ppermute | solution.py:476
  7.0 3.3 %collective-permute-start.2 = (f32[1,256]{1,0:T(1,128)S(1)}, f32[1,256]{1,0:T(1,128)S(1)}, u32[]{:S(2)}, u32[]{:S(2)}) collective-permute-start(f32[1,256]{1,0:T(1,128)S(1)} %constant_dynamic-update-slice_fusion), channel_id=1, source_target_pairs={{19,0},{3,1},{21,2},{5,3},{23,4},{7,5},{25,6},{9,7},{27,8},{11,9},... | collective-permute-start | bytes 3080 | tf_op jit(solution)/shard_map/ppermute | solution.py:476
  7.0 3.3 %collective-permute-start.1 = (f32[1,256]{1,0:T(1,128)S(1)}, f32[1,256]{1,0:T(1,128)S(1)}, u32[]{:S(2)}, u32[]{:S(2)}) collective-permute-start(f32[1,256]{1,0:T(1,128)S(1)} %constant_dynamic-update-slice_fusion), channel_id=1, source_target_pairs={{18,0},{2,1},{20,2},{4,3},{22,4},{6,5},{24,6},{8,7},{26,8},{10,9},... | collective-permute-start | bytes 3080 | tf_op jit(solution)/shard_map/ppermute | solution.py:476
  9.6 0.7 collective-permute-start
  10.3 13.5 %collective-permute-start.6 = (f32[4,256]{1,0:T(4,128)S(1)}, f32[4,256]{1,0:T(4,128)S(1)}, u32[]{:S(2)}, u32[]{:S(2)}) collective-permute-start(f32[4,256]{1,0:T(4,128)S(1)} %pad_maximum_fusion), channel_id=1, source_target_pairs={{12,0},{13,1},{14,2},{15,3},{1,4},{0,5},{3,6},{2,7},{5,8},{4,9},{7... | collective-permute-start | bytes 12296 | tf_op jit(solution)/shard_map/ppermute | solution.py:486
  15.8 8.1 %collective-permute-start.5 = (f32[4,256]{1,0:T(4,128)S(1)}, f32[4,256]{1,0:T(4,128)S(1)}, u32[]{:S(2)}, u32[]{:S(2)}) collective-permute-start(f32[4,256]{1,0:T(4,128)S(1)} %pad_maximum_fusion), channel_id=1, source_target_pairs={{8,0},{9,1},{10,2},{11,3},{12,4},{13,5},{14,6},{15,7},{1,8},{0,9},... | collective-permute-start | bytes 12296 | tf_op jit(solution)/shard_map/ppermute | solution.py:486
  15.8 8.1 %collective-permute-start.4 = (f32[4,256]{1,0:T(4,128)S(1)}, f32[4,256]{1,0:T(4,128)S(1)}, u32[]{:S(2)}, u32[]{:S(2)}) collective-permute-start(f32[4,256]{1,0:T(4,128)S(1)} %pad_maximum_fusion), channel_id=1, source_target_pairs={{4,0},{5,1},{6,2},{7,3},{8,4},{9,5},{10,6},{11,7},{12,8},{13,9},{1... | collective-permute-start | bytes 12296 | tf_op jit(solution)/shard_map/ppermute | solution.py:486
  18.3 0.9 copy-start
  19.3 0.9 copy-start.2
  20.2 0.9 copy-start.3
  21.2 0.9 copy-start.4
  22.1 1.8 %copy-start.1 = (f32[256,256]{1,0:T(8,128)S(1)}, f32[256,256]{1,0:T(8,128)}, u32[]{:S(2)}) copy-start(f32[256,256]{1,0:T(8,128)} %noise_ref.3) | copy-start | bytes 786436
  23.9 0.7 copy-start.5
  120.9 2.4 %collective-permute-start.7 = (f32[528,256]{1,0:T(8,128)S(1)}, f32[528,256]{1,0:T(8,128)S(1)}, u32[]{:S(2)}, u32[]{:S(2)}) collective-permute-start(f32[528,256]{1,0:T(8,128)S(1)} %get-tuple-element.16.state_ref), channel_id=1, source_target_pairs={{0,1},{1,0},{2,3},{3,2},{4,5},{5,4},{6,7},{7,6},{8,9},{9,8},{10,11... | collective-permute-start | bytes 1622024 | tf_op jit(solution)/shard_map/ppermute | solution.py:551
  121.0 2.3 %collective-permute-start.8 = (f32[272,256]{1,0:T(8,128)S(1)}, f32[272,256]{1,0:T(8,128)S(1)}, u32[]{:S(2)}, u32[]{:S(2)}) collective-permute-start(f32[272,256]{1,0:T(8,128)S(1)} %get-tuple-element.17.info_ref), channel_id=1, source_target_pairs={{0,1},{1,0},{2,3},{3,2},{4,5},{5,4},{6,7},{7,6},{8,9},{9,8},{10,11... | collective-permute-start | bytes 835592 | tf_op jit(solution)/shard_map/ppermute | solution.py:552
  148.7 11.5 %collective-permute-start.10 = (f32[1,256,256]{2,1,0:T(8,128)S(1)}, f32[1,256,256]{2,1,0:T(8,128)S(1)}, u32[]{:S(2)}, u32[]{:S(2)}) collective-permute-start(f32[1,256,256]{2,1,0:T(8,128)S(1)} %get-tuple-element.19), channel_id=1, source_target_pairs={{0,0},{1,16},{2,2},{3,18},{4,4},{5,20},{6,6},{7,22},{8,8},{9,24},{... | collective-permute-start | bytes 786440 | tf_op jit(solution)/shard_map/ppermute | solution.py:566
  153.2 7.1 %collective-permute-start.9 = (f32[1,256]{1,0:T(1,128)S(1)}, f32[1,256]{1,0:T(1,128)S(1)}, u32[]{:S(2)}, u32[]{:S(2)}) collective-permute-start(f32[1,256]{1,0:T(1,128)S(1)} %get-tuple-element.18), channel_id=1, source_target_pairs={{0,0},{1,16},{2,2},{3,18},{4,4},{5,20},{6,6},{7,22},{8,8},{9,24},{... | collective-permute-start | bytes 3080 | tf_op jit(solution)/shard_map/ppermute | solution.py:566

commit v5 on v2

--- a/solution.py
+++ b/solution.py
@@ -10,9 +10,12 @@
 ROWS = 8
 LANES = 128
 VECTOR = 16
+GROUP = 8
+LEAD = 2
 EXTRA = ROWS + ROWS // 2
 BOARD = ROWS * (EXTRA + ROWS)
 FAN = 4
+DIRECT = 4
 
 
 def dot_nn(left, right):
@@ -79,6 +82,17 @@
     return jnp.broadcast_to(x[:, lane : lane + 1], x.shape)
 
 
+def exact_tn(left, right):
+    a, b, c = pieces(left, 3)
+    p, q, r = pieces(right, 3)
+    return lax.dot_general(
+        jnp.concatenate([a, a, b, a, b, c], axis=0),
+        jnp.concatenate([p, q, p, r, q, p], axis=0),
+        (((0,), (0,)), ((), ())),
+        preferred_element_type=jnp.float32,
+    )
+
+
 def exact_nt(left, right):
     a, b, c = pieces(left, 3)
     p, q, r = pieces(right, 3)
@@ -104,9 +118,10 @@
     return join_nt(left_of(left), right_of(right))
 
 
-def factor_small(matrices, board):
+def factor_small(matrices, board, group=None):
     side = matrices[0].shape[0]
     count = side // ROWS
+    group = group or count
     shape = (ROWS, side)
     row = lax.broadcasted_iota(jnp.int32, shape, 0)
     lane = lax.broadcasted_iota(jnp.int32, shape, 1)
@@ -116,6 +131,8 @@
     for k in range(count):
         base = ROWS * k
         more = k + 1 < count
+        stop = min(count, (k // group + 1) * group)
+        reach = min(count, stop + LEAD)
         for t, (X, out) in enumerate(zip(tasks, outs)):
 
             def put(slot, values):
@@ -182,7 +199,7 @@
                     for q in rest:
                         nexts[q] = nexts[q] - h0 * firsts[q] - h1 * seconds[q]
                     X[k + 1] = jnp.where(pair, 0.0, X[k + 1]) - h0 * xp - h1 * xq
-                for j in range(k + 2, count):
+                for j in range(k + 2, reach):
                     g0 = spread_lane(X[j], p)
                     g1 = spread_lane(X[j], p + 1) - ratio * g0
                     X[j] = jnp.where(pair, 0.0, X[j]) - g0 * xp_scaled - g1 * xq_scaled
@@ -192,13 +209,23 @@
             diagonal = jnp.where(lane == row + base, pivots * s, 0.0)
             out[0].append(jnp.where(lane > row + base, scaled, diagonal))
             out[1].append(jnp.where(lane <= row + base, scaled, 0.0))
+            if k + 1 == stop and reach < count:
+                begin = stop - group
+                low, high = ROWS * begin, ROWS * stop
+                uppers = jnp.concatenate(out[0][begin:stop], axis=0)
+                lowers = jnp.concatenate(out[1][begin:stop], axis=0)
+                after = lax.broadcasted_iota(jnp.int32, uppers.shape, 1) >= high
+                change = exact_tn(uppers, jnp.where(after, uppers, lowers))
+                here = (lane >= low) & (lane < high)
+                for j in range(reach, count):
+                    X[j] = jnp.where(here, 0.0, X[j]) - change[ROWS * j : ROWS * (j + 1)]
     return [(jnp.concatenate(u, axis=0), jnp.concatenate(v, axis=0)) for u, v in outs]
 
 
 def factor(matrices, board):
     blocks = matrices[0].shape[0] // LANES
     if blocks == 1:
-        return factor_small(matrices, board)
+        return factor_small(matrices, board, GROUP)
 
     def cut(m, i, j):
         return m[LANES * i : LANES * (i + 1), LANES * j : LANES * (j + 1)]
@@ -215,7 +242,7 @@
                 head = head - exact_nt(L[j, k], L[j, k])
             heads.append(head)
         for m, U, L, V, (u, v) in zip(
-            matrices, uppers, lowers, inverses, factor_small(heads, board)
+            matrices, uppers, lowers, inverses, factor_small(heads, board, GROUP)
         ):
             U[j, j] = u
             V[j, j] = v
@@ -364,7 +391,7 @@
 
 
 def meet_kernel(
-    role_ref, state_ref, info_ref, far_state_ref, far_info_ref, mean_ref, cov_ref, board
+    role_ref, state_ref, info_ref, far_state_ref, far_info_ref, packed_ref, board
 ):
     n = state_ref.shape[1]
     late = role_ref[0] == 1
@@ -410,9 +437,39 @@
     early_root = near_nt(cut_root_t, last)
     early_center = cut_center + near_nt(near_nn(pull, early_root), early_root)
     root = near_nt(jnp.where(late, late_root, cut_root_t), last)
-    cov_ref[0] = jnp.where(late, leftover, 0.0) + near_nt(root, root)
+    cov = jnp.where(late, leftover, 0.0) + near_nt(root, root)
     late_center = near_nn(early_center, through) + through_center
-    mean_ref[...] = jnp.where(late, late_center, early_center)[0:1]
+    mean = jnp.where(late, late_center, early_center)[0:1]
+    half = n // 2
+    row, col = square(half)
+    last_block = cov[half:, half:]
+    diagonal = jnp.sum(jnp.where(row == col, last_block, 0.0), axis=0, keepdims=True)
+    packed_ref[0:half, 0:half] = jnp.where(row >= col, cov[0:half, 0:half], last_block)
+    packed_ref[0:half, half:] = cov[0:half, half:]
+    line = lax.broadcasted_iota(jnp.int32, (ROWS, n), 0)
+    diagonal = jnp.concatenate([diagonal, jnp.zeros_like(diagonal)], axis=1)
+    packed_ref[half:] = jnp.where(line == 0, mean, jnp.where(line == 1, diagonal, 0.0))
+
+
+def square(side):
+    return (
+        lax.broadcasted_iota(jnp.int32, (side, side), 0),
+        lax.broadcasted_iota(jnp.int32, (side, side), 1),
+    )
+
+
+def unfold_kernel(packed_ref, mean_ref, cov_ref):
+    half = packed_ref.shape[1] // 2
+    row, col = square(half)
+    both = packed_ref[0:half, 0:half]
+    across = packed_ref[0:half, half:]
+    above = jnp.where(row < col, both, 0.0)
+    cov_ref[0, 0:half, 0:half] = jnp.where(row >= col, both, 0.0) + jnp.where(row > col, both, 0.0).T
+    cov_ref[0, 0:half, half:] = across
+    cov_ref[0, half:, 0:half] = across.T
+    diagonal = jnp.where(row == col, packed_ref[half + 1 : half + 2, 0:half], 0.0)
+    cov_ref[0, half:, half:] = above + above.T + diagonal
+    mean_ref[...] = packed_ref[half : half + 1]
 
 
 def begin_of(device, devices):
@@ -428,7 +485,7 @@
     devices = lax.axis_size(axis)
     begins = [begin_of(i, devices) for i in range(devices)]
     holder = {begin: i for i, begin in enumerate(begins)}
-    held = min(FAN, steps)
+    held = min(DIRECT, steps)
     parts = [
         lax.ppermute(rows, axis, [((begins[i] + j) % devices, i) for i in range(devices)])
         for j in range(held)
@@ -490,11 +547,11 @@
     swap = [(i, i ^ 1) for i in range(devices)]
     far_state = lax.ppermute(state, "tm", swap)
     far_info = lax.ppermute(info, "tm", swap)
-    mean, cov = pl.pallas_call(
+    packed = pl.pallas_call(
         meet_kernel,
-        out_shape=(shape(1, n), shape(1, n, n)),
+        out_shape=shape(n // 2 + ROWS, n),
         in_specs=[smem] + [vmem] * 4,
-        out_specs=(vmem, vmem),
+        out_specs=vmem,
         scratch_shapes=[pltpu.VMEM((1, 2, BOARD, LANES), jnp.float32)],
         compiler_params=params,
     )(role.reshape(1), state, info, far_state, far_info)
@@ -503,7 +560,13 @@
         above = i >= half
         spot = 2 * ((i - half if above else i) // 2) + (1 if above else 0)
         home.append((i, spot + half if i % 2 else spot))
-    return lax.ppermute(mean, "tm", home), lax.ppermute(cov, "tm", home)
+    return pl.pallas_call(
+        unfold_kernel,
+        out_shape=(shape(1, n), shape(1, n, n)),
+        in_specs=[vmem],
+        out_specs=(vmem, vmem),
+        compiler_params=params,
+    )(lax.ppermute(packed, "tm", home))
 
 
 def solution(mesh):

time: 157 us -> 153 us (0.975)
  starting transfers between devices: 23.9 us -> 21.9 us
    ppermute x2 -> x1, starting transfers between devices: 6.46 us -> 4.4 us  [shards(): lax.ppermute(packed, 'tm', home)]
    unnamed x15 -> x13, local copies, waits for them, and re-layouts: 5.41 us -> 4.14 us
    ppermute x2 -> x1, waiting for transfers between devices: 4.98 us -> 4.36 us  [shards(): lax.ppermute(packed, 'tm', home)]
    pallas_call x1 -> x2, Pallas kernels: 25.4 us -> 25.2 us  [the longest x1 24.4 us: shards(): pl.pallas_call(meet_kernel, out_shape=shape(n // 2 + ROWS, n), in_specs=[...]
  transfers between devices with their start and end apart: 11 -> 10, of which waited for: 2 -> 2; matrix products, arithmetic and copies ran while one was open for 0% -> 0% of each run, Pallas kernels for 1% -> 1%
where the time goes in v5:
time: 153 us; the launch traced here: 152 us
  Pallas kernels  119 us (78%)
  starting transfers between devices  21.9 us (14%)
  waiting for transfers between devices  6.25 us (4%)
  local copies, waits for them, and re-layouts  4.19 us (3%)
    pallas_call x1, Pallas kernels, shards(): pl.pallas_call(functools.partial(window_kernel, half, devices), out_shape...  93.2 us
    pallas_call x1, Pallas kernels, shards(): pl.pallas_call(meet_kernel, out_shape=shape(n // 2 + ROWS, n), in_specs=[...  24.4 us
    ppermute x4, starting transfers between devices, gather_rows(): lax.ppermute(rows, axis, [((begins[i] + j) % devices, i) for i in range(d...  8.93 us
    ppermute x3, starting transfers between devices, gather_rows(): parts.append(lax.ppermute(rows[:size], axis, pairs))  7.98 us
    ppermute x1, starting transfers between devices, shards(): lax.ppermute(packed, 'tm', home)  4.4 us
    ppermute x1, waiting for transfers between devices, shards(): lax.ppermute(packed, 'tm', home)  4.36 us
    unnamed x13, local copies, waits for them, and re-layouts  4.14 us
  transfers between devices with their start and end apart: 10, of which 2 were waited for; matrix products, arithmetic and copies ran while one was open for 0% of the time, Pallas kernels for 1%

profile of v5, /device:TPU:1, one launch (start us, length us, event | category | flops | bytes accessed | tf_op | source)
XLA Modules:
  0.0 152.4 jit_solution(4963855412056832607)
XLA Ops:
  0.6 0.0 copy-start.5
  0.6 0.7 constant_dynamic-update-slice_fusion.1
  1.3 0.0 copy-done.5
  1.3 5.7 %collective-permute-start.3 = (f32[1,256]{1,0:T(1,128)S(1)}, f32[1,256]{1,0:T(1,128)S(1)}, u32[]{:S(2)}, u32[]{:S(2)}) collective-permute-start(f32[1,256]{1,0:T(1,128)S(1)} %constant_dynamic-update-slice_fusion), channel_id=1, source_target_pairs={{20,0},{4,1},{22,2},{6,3},{24,4},{8,5},{26,6},{10,7},{28,8},{12,9}... | collective-permute-start | bytes 3080 | tf_op jit(solution)/shard_map/ppermute | solution.py:490
  7.0 0.0 collective-permute-start.2
  7.0 2.6 %collective-permute-start.1 = (f32[1,256]{1,0:T(1,128)S(1)}, f32[1,256]{1,0:T(1,128)S(1)}, u32[]{:S(2)}, u32[]{:S(2)}) collective-permute-start(f32[1,256]{1,0:T(1,128)S(1)} %constant_dynamic-update-slice_fusion), channel_id=1, source_target_pairs={{18,0},{2,1},{20,2},{4,3},{22,4},{6,5},{24,6},{8,7},{26,8},{10,9},... | collective-permute-start | bytes 3080 | tf_op jit(solution)/shard_map/ppermute | solution.py:490
  9.6 0.6 collective-permute-start
  10.3 0.0 collective-permute-done.3
  10.3 0.0 collective-permute-done.2
  10.3 0.0 collective-permute-done.1
  10.3 0.0 collective-permute-done
  10.3 5.4 %collective-permute-start.6 = (f32[4,256]{1,0:T(4,128)S(1)}, f32[4,256]{1,0:T(4,128)S(1)}, u32[]{:S(2)}, u32[]{:S(2)}) collective-permute-start(f32[4,256]{1,0:T(4,128)S(1)} %pad_maximum_fusion), channel_id=1, source_target_pairs={{12,0},{13,1},{14,2},{15,3},{1,4},{0,5},{3,6},{2,7},{5,8},{4,9},{7... | collective-permute-start | bytes 12296 | tf_op jit(solution)/shard_map/ppermute | solution.py:500
  15.8 0.0 collective-permute-start.5
  15.8 2.6 %collective-permute-start.4 = (f32[4,256]{1,0:T(4,128)S(1)}, f32[4,256]{1,0:T(4,128)S(1)}, u32[]{:S(2)}, u32[]{:S(2)}) collective-permute-start(f32[4,256]{1,0:T(4,128)S(1)} %pad_maximum_fusion), channel_id=1, source_target_pairs={{4,0},{5,1},{6,2},{7,3},{8,4},{9,5},{10,6},{11,7},{12,8},{13,9},{1... | collective-permute-start | bytes 12296 | tf_op jit(solution)/shard_map/ppermute | solution.py:500
  18.3 0.0 copy-start.1
  18.3 0.9 copy-done.1
  19.3 0.0 copy-start.2
  19.3 0.9 copy-done.2
  20.2 0.0 copy-start.3
  20.2 0.9 copy-done.3
  21.1 0.0 copy-start
  21.1 0.9 shard_map.86
  22.1 0.0 collective-permute-done.6
  22.1 0.0 collective-permute-done.5
  22.1 0.0 collective-permute-done.4
  22.1 0.0 copy-start.4
  22.1 0.0 copy-done
  22.1 0.7 copy-done.4
  22.8 93.2 %shard_map.87 = (f32[528,256]{1,0:T(8,128)S(1)}, f32[272,256]{1,0:T(8,128)S(1)}) custom-call(s32[1]{0:T(128)} %bitcast.1.begin_ref, f32[16,256]{1,0:T(8,128)S(1)} %concatenate.12.rows_ref, bf16[384,1024]{1,0:T(8,128)(2,1)S(1)} %get-tuple-element.7.left_ref, bf16[384,1024]{1,0:T(8,128)(2,1)S(1)} %get-tuple-element.8.right_ref, ...), custom_call_target="tpu_custom_call" | custom-call | tf_op jit(solution)/shard_map/pallas_call | solution.py:533
  116.1 0.1 collective-permute-start.7
  116.1 0.5 collective-permute-start.8
  116.6 1.8 %collective-permute-done.8.far_info_ref = f32[272,256]{1,0:T(8,128)S(1)} collective-permute-done((f32[272,256]{1,0:T(8,128)S(1)}, f32[272,256]{1,0:T(8,128)S(1)}, u32[]{:S(2)}, u32[]{:S(2)}) %collective-permute-start.8) | collective-permute-done | bytes 278560 | tf_op jit(solution)/shard_map/ppermute | solution.py:549
  118.5 0.0 collective-permute-done.7.far_state_ref
  118.5 24.4 %shard_map.88 = f32[136,256]{1,0:T(8,128)S(1)} custom-call(s32[1]{0:T(128)} %bitcast.role_ref, f32[528,256]{1,0:T(8,128)S(1)} %get-tuple-element.10.state_ref, f32[272,256]{1,0:T(8,128)S(1)} %get-tuple-element.11.info_ref, f32[528,256]{1,0:T(8,128)S(1)} %collective-permute-done.7.far_state_ref, f32[272,256]{1,0:T(8,128)S(1)} %collective-permute-done.8.far_info_ref), custom_call_target="tpu_custom_call" | custom-call | tf_op jit(solution)/shard_map/pallas_call | solution.py:550
  142.8 4.4 %collective-permute-start.9 = (f32[136,256]{1,0:T(8,128)S(1)}, f32[136,256]{1,0:T(8,128)S(1)}, u32[]{:S(2)}, u32[]{:S(2)}) collective-permute-start(f32[136,256]{1,0:T(8,128)S(1)} %shard_map.88), channel_id=1, source_target_pairs={{0,0},{1,16},{2,2},{3,18},{4,4},{5,20},{6,6},{7,22},{8,8},{9,24},{... | collective-permute-start | bytes 417800 | tf_op jit(solution)/shard_map/ppermute | solution.py:569
  147.2 4.4 %collective-permute-done.9.packed_ref = f32[136,256]{1,0:T(8,128)S(1)} collective-permute-done((f32[136,256]{1,0:T(8,128)S(1)}, f32[136,256]{1,0:T(8,128)S(1)}, u32[]{:S(2)}, u32[]{:S(2)}) %collective-permute-start.9) | collective-permute-done | bytes 139296 | tf_op jit(solution)/shard_map/ppermute | solution.py:569
  151.6 0.8 shard_map.89
  (3 shorter events, 0.1 us)
Async XLA Ops:
  0.6 0.7 copy-start.5
  1.3 8.9 %collective-permute-start.3 = (f32[1,256]{1,0:T(1,128)S(1)}, f32[1,256]{1,0:T(1,128)S(1)}, u32[]{:S(2)}, u32[]{:S(2)}) collective-permute-start(f32[1,256]{1,0:T(1,128)S(1)} %constant_dynamic-update-slice_fusion), channel_id=1, source_target_pairs={{20,0},{4,1},{22,2},{6,3},{24,4},{8,5},{26,6},{10,7},{28,8},{12,9}... | collective-permute-start | bytes 3080 | tf_op jit(solution)/shard_map/ppermute | solution.py:490
  7.0 3.3 %collective-permute-start.2 = (f32[1,256]{1,0:T(1,128)S(1)}, f32[1,256]{1,0:T(1,128)S(1)}, u32[]{:S(2)}, u32[]{:S(2)}) collective-permute-start(f32[1,256]{1,0:T(1,128)S(1)} %constant_dynamic-update-slice_fusion), channel_id=1, source_target_pairs={{19,0},{3,1},{21,2},{5,3},{23,4},{7,5},{25,6},{9,7},{27,8},{11,9},... | collective-permute-start | bytes 3080 | tf_op jit(solution)/shard_map/ppermute | solution.py:490
  7.0 3.3 %collective-permute-start.1 = (f32[1,256]{1,0:T(1,128)S(1)}, f32[1,256]{1,0:T(1,128)S(1)}, u32[]{:S(2)}, u32[]{:S(2)}) collective-permute-start(f32[1,256]{1,0:T(1,128)S(1)} %constant_dynamic-update-slice_fusion), channel_id=1, source_target_pairs={{18,0},{2,1},{20,2},{4,3},{22,4},{6,5},{24,6},{8,7},{26,8},{10,9},... | collective-permute-start | bytes 3080 | tf_op jit(solution)/shard_map/ppermute | solution.py:490
  9.6 0.7 collective-permute-start
  10.3 11.7 %collective-permute-start.6 = (f32[4,256]{1,0:T(4,128)S(1)}, f32[4,256]{1,0:T(4,128)S(1)}, u32[]{:S(2)}, u32[]{:S(2)}) collective-permute-start(f32[4,256]{1,0:T(4,128)S(1)} %pad_maximum_fusion), channel_id=1, source_target_pairs={{12,0},{13,1},{14,2},{15,3},{1,4},{0,5},{3,6},{2,7},{5,8},{4,9},{7... | collective-permute-start | bytes 12296 | tf_op jit(solution)/shard_map/ppermute | solution.py:500
  15.8 6.3 %collective-permute-start.5 = (f32[4,256]{1,0:T(4,128)S(1)}, f32[4,256]{1,0:T(4,128)S(1)}, u32[]{:S(2)}, u32[]{:S(2)}) collective-permute-start(f32[4,256]{1,0:T(4,128)S(1)} %pad_maximum_fusion), channel_id=1, source_target_pairs={{8,0},{9,1},{10,2},{11,3},{12,4},{13,5},{14,6},{15,7},{1,8},{0,9},... | collective-permute-start | bytes 12296 | tf_op jit(solution)/shard_map/ppermute | solution.py:500
  15.8 6.3 %collective-permute-start.4 = (f32[4,256]{1,0:T(4,128)S(1)}, f32[4,256]{1,0:T(4,128)S(1)}, u32[]{:S(2)}, u32[]{:S(2)}) collective-permute-start(f32[4,256]{1,0:T(4,128)S(1)} %pad_maximum_fusion), channel_id=1, source_target_pairs={{4,0},{5,1},{6,2},{7,3},{8,4},{9,5},{10,6},{11,7},{12,8},{13,9},{1... | collective-permute-start | bytes 12296 | tf_op jit(solution)/shard_map/ppermute | solution.py:500
  18.3 0.9 copy-start.1
  19.3 0.9 copy-start.2
  20.2 0.9 copy-start.3
  21.1 1.0 copy-start
  22.1 0.7 copy-start.4
  116.1 2.4 %collective-permute-start.7 = (f32[528,256]{1,0:T(8,128)S(1)}, f32[528,256]{1,0:T(8,128)S(1)}, u32[]{:S(2)}, u32[]{:S(2)}) collective-permute-start(f32[528,256]{1,0:T(8,128)S(1)} %get-tuple-element.10.state_ref), channel_id=1, source_target_pairs={{0,1},{1,0},{2,3},{3,2},{4,5},{5,4},{6,7},{7,6},{8,9},{9,8},{10,11... | collective-permute-start | bytes 1622024 | tf_op jit(solution)/shard_map/ppermute | solution.py:548
  116.1 2.3 %collective-permute-start.8 = (f32[272,256]{1,0:T(8,128)S(1)}, f32[272,256]{1,0:T(8,128)S(1)}, u32[]{:S(2)}, u32[]{:S(2)}) collective-permute-start(f32[272,256]{1,0:T(8,128)S(1)} %get-tuple-element.11.info_ref), channel_id=1, source_target_pairs={{0,1},{1,0},{2,3},{3,2},{4,5},{5,4},{6,7},{7,6},{8,9},{9,8},{10,11... | collective-permute-start | bytes 835592 | tf_op jit(solution)/shard_map/ppermute | solution.py:549
  142.8 8.8 %collective-permute-start.9 = (f32[136,256]{1,0:T(8,128)S(1)}, f32[136,256]{1,0:T(8,128)S(1)}, u32[]{:S(2)}, u32[]{:S(2)}) collective-permute-start(f32[136,256]{1,0:T(8,128)S(1)} %shard_map.88), channel_id=1, source_target_pairs={{0,0},{1,16},{2,2},{3,18},{4,4},{5,20},{6,6},{7,22},{8,8},{9,24},{... | collective-permute-start | bytes 417800 | tf_op jit(solution)/shard_map/ppermute | solution.py:569

commit v6 on v5

--- a/solution.py
+++ b/solution.py
@@ -14,8 +14,6 @@
 LEAD = 2
 EXTRA = ROWS + ROWS // 2
 BOARD = ROWS * (EXTRA + ROWS)
-FAN = 4
-DIRECT = 4
 
 
 def dot_nn(left, right):
@@ -330,7 +328,7 @@
         return jnp.where(t >= times, t - times, t)
 
     def line_at(k):
-        return rows_ref[pl.ds(jnp.minimum(k, steps - 1), 1), :]
+        return rows_ref[pl.ds(wrap(begin + jnp.minimum(k, steps - 1)), 1), :]
 
     def first_spread(k, spread):
         line = line_at(k)
@@ -481,26 +479,11 @@
     return (split + 1 + (1 - role) * (devices - devices // 2)) % devices
 
 
-def gather_rows(rows, steps, axis):
+def gather_rows(rows, axis):
     devices = lax.axis_size(axis)
-    begins = [begin_of(i, devices) for i in range(devices)]
-    holder = {begin: i for i, begin in enumerate(begins)}
-    held = min(DIRECT, steps)
-    parts = [
-        lax.ppermute(rows, axis, [((begins[i] + j) % devices, i) for i in range(devices)])
-        for j in range(held)
-    ]
-    rows = jnp.concatenate(parts, axis=0)
-    while held < steps:
-        parts = [rows]
-        for m in range(1, FAN):
-            size = min(held, steps - m * held)
-            if size > 0:
-                pairs = [(holder[(begins[i] + m * held) % devices], i) for i in range(devices)]
-                parts.append(lax.ppermute(rows[:size], axis, pairs))
-        rows = jnp.concatenate(parts, axis=0)
-        held = min(steps, FAN * held)
-    return rows
+    return lax.all_to_all(
+        jnp.broadcast_to(rows, (devices, rows.shape[1])), axis, 0, 0, tiled=True
+    )
 
 
 def shards(
@@ -514,7 +497,7 @@
     role = device % 2
     begin = begin_of(device, devices)
 
-    rows = gather_rows(jnp.concatenate([measurements, noise_levels], axis=1), half, "tm")
+    rows = gather_rows(jnp.concatenate([measurements, noise_levels], axis=1), "tm")
     vmem = pl.BlockSpec(memory_space=pltpu.VMEM)
     smem = pl.BlockSpec(memory_space=pltpu.SMEM)
     params = pltpu.CompilerParams(vmem_limit_bytes=48 * 1024 * 1024)

time: 153 us -> 147 us (0.961)
  starting transfers between devices: 21.9 us -> 10.2 us
  waiting for transfers between devices: 6.25 us -> 12.3 us
    ppermute x7 -> x0, starting transfers between devices: 16.9 us -> none  [the longest x4 8.93 us: gather_rows(): lax.ppermute(rows, axis, [((begins[i] + j) % devices, i) for i in range(d...]
    all_to_all x0 -> x1, starting transfers between devices: none -> 7.1 us  [gather_rows(): lax.all_to_all(jnp.broadcast_to(rows, (devices, rows.shape[1])), axis, 0,...]
    all_to_all x0 -> x1, waiting for transfers between devices: none -> 4.21 us  [gather_rows(): lax.all_to_all(jnp.broadcast_to(rows, (devices, rows.shape[1])), axis, 0,...]
    ppermute x1, waiting for transfers between devices: 4.36 us -> 6.25 us  [shards(): lax.ppermute(packed, 'tm', home)]
    ppermute x1, starting transfers between devices: 4.4 us -> 2.51 us  [shards(): lax.ppermute(packed, 'tm', home)]
    unnamed x13 -> x11, local copies, waits for them, and re-layouts: 4.14 us -> 2.58 us
  transfers between devices with their start and end apart: 10 -> 4, of which waited for: 2 -> 3; matrix products, arithmetic and copies ran while one was open for 0% -> 0% of each run, Pallas kernels for 1% -> 1%
where the time goes in v6:
time: 147 us
  Pallas kernels  119 us (81%)
  waiting for transfers between devices  12.3 us (8%)
  starting transfers between devices  10.2 us (7%)
  local copies, waits for them, and re-layouts  3.21 us (2%)
    pallas_call x1, Pallas kernels, shards(): pl.pallas_call(functools.partial(window_kernel, half, devices), out_shape...  93.2 us
    pallas_call x1, Pallas kernels, shards(): pl.pallas_call(meet_kernel, out_shape=shape(n // 2 + ROWS, n), in_specs=[...  24.4 us
    all_to_all x1, starting transfers between devices, gather_rows(): lax.all_to_all(jnp.broadcast_to(rows, (devices, rows.shape[1])), axis, 0,...  7.1 us
    ppermute x1, waiting for transfers between devices, shards(): lax.ppermute(packed, 'tm', home)  6.25 us
    all_to_all x1, waiting for transfers between devices, gather_rows(): lax.all_to_all(jnp.broadcast_to(rows, (devices, rows.shape[1])), axis, 0,...  4.21 us
  transfers between devices with their start and end apart: 4, of which 3 were waited for; matrix products, arithmetic and copies ran while one was open for 0% of the time, Pallas kernels for 1%

profile of v6, /device:TPU:1, one launch (start us, length us, event | category | flops | bytes accessed | tf_op | source)
XLA Modules:
  0.0 146.5 jit_solution(3725209727457397)
XLA Ops:
  0.6 0.0 copy-start.3
  0.6 0.7 pad_maximum_fusion
  1.4 0.6 broadcast_in_dim.2
  2.0 7.1 %all-to-all-start = ((f32[32,1,256]{2,1,0:T(1,128)}), f32[32,1,256]{2,1,0:T(1,128)S(1)}, u32[]{:S(2)}, u32[]{:S(2)}) async-start(f32[32,1,256]{2,1,0:T(1,128)} %broadcast_in_dim.2), calls=%async_computation | async-start | bytes 65536 | tf_op jit(solution)/shard_map/all_to_all | solution.py:484
  9.1 0.0 copy-done.3
  9.2 0.0 copy-start.1
  9.2 0.9 copy-done.1
  10.1 0.0 copy-start.2
  10.1 0.9 copy-done.2
  11.1 0.0 copy-start
  11.1 0.9 shard_map.86
  12.0 4.2 %all-to-all-done = f32[32,1,256]{2,1,0:T(1,128)S(1)} async-done(((f32[32,1,256]{2,1,0:T(1,128)}), f32[32,1,256]{2,1,0:T(1,128)S(1)}, u32[]{:S(2)}, u32[]{:S(2)}) %all-to-all-start) | async-done | bytes 32800 | tf_op jit(solution)/shard_map/all_to_all | solution.py:484
  16.2 0.0 copy-start.4
  16.2 0.0 copy-done
  16.2 0.7 copy-done.4
  16.9 93.2 %shard_map.87 = (f32[528,256]{1,0:T(8,128)S(1)}, f32[272,256]{1,0:T(8,128)S(1)}) custom-call(s32[1]{0:T(128)} %bitcast.1.begin_ref, f32[32,256]{1,0:T(8,128)S(1)} %bitcast.7, bf16[384,1024]{1,0:T(8,128)(2,1)S(1)} %get-tuple-element.7.left_ref, bf16[384,1024]{1,0:T(8,128)(2,1)S(1)} %get-tuple-element.8.right_ref, f32[384,384]{1,0:T(8,128)S(1)} %get-tuple-element.9.consts_ref, ...), custom_call_target="tpu_custom_call" | custom-call | tf_op jit(solution)/shard_map/pallas_call | solution.py:516
  110.1 0.5 collective-permute-start
  110.6 0.1 collective-permute-start.1
  110.7 1.8 %collective-permute-done.1.far_info_ref = f32[272,256]{1,0:T(8,128)S(1)} collective-permute-done((f32[272,256]{1,0:T(8,128)S(1)}, f32[272,256]{1,0:T(8,128)S(1)}, u32[]{:S(2)}, u32[]{:S(2)}) %collective-permute-start.1) | collective-permute-done | bytes 278560 | tf_op jit(solution)/shard_map/ppermute | solution.py:532
  112.6 0.0 collective-permute-done.far_state_ref
  112.6 24.4 %shard_map.88 = f32[136,256]{1,0:T(8,128)S(1)} custom-call(s32[1]{0:T(128)} %bitcast.role_ref, f32[528,256]{1,0:T(8,128)S(1)} %get-tuple-element.10.state_ref, f32[272,256]{1,0:T(8,128)S(1)} %get-tuple-element.11.info_ref, f32[528,256]{1,0:T(8,128)S(1)} %collective-permute-done.far_state_ref, f32[272,256]{1,0:T(8,128)S(1)} %collective-permute-done.1.far_info_ref), custom_call_target="tpu_custom_call" | custom-call | tf_op jit(solution)/shard_map/pallas_call | solution.py:533
  136.9 2.5 %collective-permute-start.2 = (f32[136,256]{1,0:T(8,128)S(1)}, f32[136,256]{1,0:T(8,128)S(1)}, u32[]{:S(2)}, u32[]{:S(2)}) collective-permute-start(f32[136,256]{1,0:T(8,128)S(1)} %shard_map.88), channel_id=1, source_target_pairs={{0,0},{1,16},{2,2},{3,18},{4,4},{5,20},{6,6},{7,22},{8,8},{9,24},{... | collective-permute-start | bytes 417800 | tf_op jit(solution)/shard_map/ppermute | solution.py:552
  139.4 6.2 %collective-permute-done.2.packed_ref = f32[136,256]{1,0:T(8,128)S(1)} collective-permute-done((f32[136,256]{1,0:T(8,128)S(1)}, f32[136,256]{1,0:T(8,128)S(1)}, u32[]{:S(2)}, u32[]{:S(2)}) %collective-permute-start.2) | collective-permute-done | bytes 139296 | tf_op jit(solution)/shard_map/ppermute | solution.py:552
  145.7 0.8 shard_map.89
  (1 shorter events, 0.0 us)
Async XLA Ops:
  0.6 8.5 %copy-start.3 = (f32[128,256]{1,0:T(8,128)S(1)}, f32[128,256]{1,0:T(8,128)}, u32[]{:S(2)}) copy-start(f32[128,256]{1,0:T(8,128)} %sensing_ref.1) | copy-start | bytes 393220
  2.0 14.2 %all-to-all-start = ((f32[32,1,256]{2,1,0:T(1,128)}), f32[32,1,256]{2,1,0:T(1,128)S(1)}, u32[]{:S(2)}, u32[]{:S(2)}) async-start(f32[32,1,256]{2,1,0:T(1,128)} %broadcast_in_dim.2), calls=%async_computation | async-start | bytes 65536 | tf_op jit(solution)/shard_map/all_to_all | solution.py:484
  9.2 1.0 copy-start.1
  10.1 0.9 copy-start.2
  11.1 5.1 %copy-start = (f32[256,256]{1,0:T(8,128)S(1)}, f32[256,256]{1,0:T(8,128)}, u32[]{:S(2)}) copy-start(f32[256,256]{1,0:T(8,128)} %prior_ref.1) | copy-start | bytes 786436
  16.2 0.7 copy-start.4
  110.1 2.4 %collective-permute-start = (f32[528,256]{1,0:T(8,128)S(1)}, f32[528,256]{1,0:T(8,128)S(1)}, u32[]{:S(2)}, u32[]{:S(2)}) collective-permute-start(f32[528,256]{1,0:T(8,128)S(1)} %get-tuple-element.10.state_ref), channel_id=1, source_target_pairs={{0,1},{1,0},{2,3},{3,2},{4,5},{5,4},{6,7},{7,6},{8,9},{9,8},{10,11... | collective-permute-start | bytes 1622024 | tf_op jit(solution)/shard_map/ppermute | solution.py:531
  110.6 2.0 %collective-permute-start.1 = (f32[272,256]{1,0:T(8,128)S(1)}, f32[272,256]{1,0:T(8,128)S(1)}, u32[]{:S(2)}, u32[]{:S(2)}) collective-permute-start(f32[272,256]{1,0:T(8,128)S(1)} %get-tuple-element.11.info_ref), channel_id=1, source_target_pairs={{0,1},{1,0},{2,3},{3,2},{4,5},{5,4},{6,7},{7,6},{8,9},{9,8},{10,11... | collective-permute-start | bytes 835592 | tf_op jit(solution)/shard_map/ppermute | solution.py:532
  136.9 8.8 %collective-permute-start.2 = (f32[136,256]{1,0:T(8,128)S(1)}, f32[136,256]{1,0:T(8,128)S(1)}, u32[]{:S(2)}, u32[]{:S(2)}) collective-permute-start(f32[136,256]{1,0:T(8,128)S(1)} %shard_map.88), channel_id=1, source_target_pairs={{0,0},{1,16},{2,2},{3,18},{4,4},{5,20},{6,6},{7,22},{8,8},{9,24},{... | collective-permute-start | bytes 417800 | tf_op jit(solution)/shard_map/ppermute | solution.py:552

commit v7 on v6

--- a/solution.py
+++ b/solution.py
@@ -10,7 +10,7 @@
 ROWS = 8
 LANES = 128
 VECTOR = 16
-GROUP = 8
+GROUP = 4
 LEAD = 2
 EXTRA = ROWS + ROWS // 2
 BOARD = ROWS * (EXTRA + ROWS)
@@ -479,11 +479,10 @@
     return (split + 1 + (1 - role) * (devices - devices // 2)) % devices
 
 
-def gather_rows(rows, axis):
+def gather_rows(parts, axis):
     devices = lax.axis_size(axis)
-    return lax.all_to_all(
-        jnp.broadcast_to(rows, (devices, rows.shape[1])), axis, 0, 0, tiled=True
-    )
+    copies = [jnp.broadcast_to(part, (devices, part.shape[1])) for part in parts]
+    return lax.all_to_all(jnp.concatenate(copies, axis=1), axis, 0, 0, tiled=True)
 
 
 def shards(
@@ -497,7 +496,7 @@
     role = device % 2
     begin = begin_of(device, devices)
 
-    rows = gather_rows(jnp.concatenate([measurements, noise_levels], axis=1), "tm")
+    rows = gather_rows([measurements, noise_levels], "tm")
     vmem = pl.BlockSpec(memory_space=pltpu.VMEM)
     smem = pl.BlockSpec(memory_space=pltpu.SMEM)
     params = pltpu.CompilerParams(vmem_limit_bytes=48 * 1024 * 1024)

time: 147 us -> 146 us (level)
  no operation moved by 1% of the time
where the time goes in v7:
time: 146 us
  Pallas kernels  119 us (82%)
  waiting for transfers between devices  12.3 us (8%)
  starting transfers between devices  10.2 us (7%)
  local copies, waits for them, and re-layouts  3.21 us (2%)
    pallas_call x1, Pallas kernels, shards(): pl.pallas_call(functools.partial(window_kernel, half, devices), out_shape...  93 us
    pallas_call x1, Pallas kernels, shards(): pl.pallas_call(meet_kernel, out_shape=shape(n // 2 + ROWS, n), in_specs=[...  24.1 us
    all_to_all x1, starting transfers between devices, gather_rows(): lax.all_to_all(jnp.concatenate(copies, axis=1), axis, 0, 0, tiled=True)  7.1 us
    ppermute x1, waiting for transfers between devices, shards(): lax.ppermute(packed, 'tm', home)  6.25 us
    all_to_all x1, waiting for transfers between devices, gather_rows(): lax.all_to_all(jnp.concatenate(copies, axis=1), axis, 0, 0, tiled=True)  4.21 us
  transfers between devices with their start and end apart: 4, of which 3 were waited for; matrix products, arithmetic and copies ran while one was open for 0% of the time, Pallas kernels for 1%

profile of v7, /device:TPU:1, one launch (start us, length us, event | category | flops | bytes accessed | tf_op | source)
XLA Modules:
  0.0 146.0 jit_solution(16570631166633249402)
XLA Ops:
  0.6 0.0 copy-start.3
  0.6 0.7 pad_maximum_fusion
  1.4 0.6 broadcast.7
  2.0 7.1 %all-to-all-start = ((f32[32,1,256]{2,1,0:T(1,128)}), f32[32,1,256]{2,1,0:T(1,128)S(1)}, u32[]{:S(2)}, u32[]{:S(2)}) async-start(f32[32,1,256]{2,1,0:T(1,128)} %broadcast.7), calls=%async_computation | async-start | bytes 65536 | tf_op jit(solution)/shard_map/all_to_all | solution.py:485
  9.2 0.0 copy-done.3
  9.2 0.0 copy-start.1
  9.2 0.9 copy-done.1
  10.1 0.0 copy-start.2
  10.1 0.9 copy-done.2
  11.1 0.0 copy-start
  11.1 0.9 shard_map.86
  12.0 4.2 %all-to-all-done = f32[32,1,256]{2,1,0:T(1,128)S(1)} async-done(((f32[32,1,256]{2,1,0:T(1,128)}), f32[32,1,256]{2,1,0:T(1,128)S(1)}, u32[]{:S(2)}, u32[]{:S(2)}) %all-to-all-start) | async-done | bytes 32800 | tf_op jit(solution)/shard_map/all_to_all | solution.py:485
  16.2 0.0 copy-start.4
  16.2 0.0 copy-done
  16.2 0.7 copy-done.4
  16.9 93.0 %shard_map.87 = (f32[528,256]{1,0:T(8,128)S(1)}, f32[272,256]{1,0:T(8,128)S(1)}) custom-call(s32[1]{0:T(128)} %bitcast.1.begin_ref, f32[32,256]{1,0:T(8,128)S(1)} %bitcast.8, bf16[384,1024]{1,0:T(8,128)(2,1)S(1)} %get-tuple-element.7.left_ref, bf16[384,1024]{1,0:T(8,128)(2,1)S(1)} %get-tuple-element.8.right_ref, f32[384,384]{1,0:T(8,128)S(1)} %get-tuple-element.9.consts_ref, ...), custom_call_target="tpu_custom_call" | custom-call | tf_op jit(solution)/shard_map/pallas_call | solution.py:515
  109.9 0.5 collective-permute-start
  110.4 0.1 collective-permute-start.1
  110.5 1.8 %collective-permute-done.1.far_info_ref = f32[272,256]{1,0:T(8,128)S(1)} collective-permute-done((f32[272,256]{1,0:T(8,128)S(1)}, f32[272,256]{1,0:T(8,128)S(1)}, u32[]{:S(2)}, u32[]{:S(2)}) %collective-permute-start.1) | collective-permute-done | bytes 278560 | tf_op jit(solution)/shard_map/ppermute | solution.py:531
  112.3 0.0 collective-permute-done.far_state_ref
  112.3 24.1 %shard_map.88 = f32[136,256]{1,0:T(8,128)S(1)} custom-call(s32[1]{0:T(128)} %bitcast.role_ref, f32[528,256]{1,0:T(8,128)S(1)} %get-tuple-element.10.state_ref, f32[272,256]{1,0:T(8,128)S(1)} %get-tuple-element.11.info_ref, f32[528,256]{1,0:T(8,128)S(1)} %collective-permute-done.far_state_ref, f32[272,256]{1,0:T(8,128)S(1)} %collective-permute-done.1.far_info_ref), custom_call_target="tpu_custom_call" | custom-call | tf_op jit(solution)/shard_map/pallas_call | solution.py:532
  136.4 2.5 %collective-permute-start.2 = (f32[136,256]{1,0:T(8,128)S(1)}, f32[136,256]{1,0:T(8,128)S(1)}, u32[]{:S(2)}, u32[]{:S(2)}) collective-permute-start(f32[136,256]{1,0:T(8,128)S(1)} %shard_map.88), channel_id=1, source_target_pairs={{0,0},{1,16},{2,2},{3,18},{4,4},{5,20},{6,6},{7,22},{8,8},{9,24},{... | collective-permute-start | bytes 417800 | tf_op jit(solution)/shard_map/ppermute | solution.py:551
  138.9 6.2 %collective-permute-done.2.packed_ref = f32[136,256]{1,0:T(8,128)S(1)} collective-permute-done((f32[136,256]{1,0:T(8,128)S(1)}, f32[136,256]{1,0:T(8,128)S(1)}, u32[]{:S(2)}, u32[]{:S(2)}) %collective-permute-start.2) | collective-permute-done | bytes 139296 | tf_op jit(solution)/shard_map/ppermute | solution.py:551
  145.2 0.8 shard_map.89
  (1 shorter events, 0.0 us)
Async XLA Ops:
  0.6 8.5 %copy-start.3 = (f32[128,256]{1,0:T(8,128)S(1)}, f32[128,256]{1,0:T(8,128)}, u32[]{:S(2)}) copy-start(f32[128,256]{1,0:T(8,128)} %sensing_ref.1) | copy-start | bytes 393220
  2.0 14.2 %all-to-all-start = ((f32[32,1,256]{2,1,0:T(1,128)}), f32[32,1,256]{2,1,0:T(1,128)S(1)}, u32[]{:S(2)}, u32[]{:S(2)}) async-start(f32[32,1,256]{2,1,0:T(1,128)} %broadcast.7), calls=%async_computation | async-start | bytes 65536 | tf_op jit(solution)/shard_map/all_to_all | solution.py:485
  9.2 1.0 copy-start.1
  10.1 0.9 copy-start.2
  11.1 5.1 %copy-start = (f32[256,256]{1,0:T(8,128)S(1)}, f32[256,256]{1,0:T(8,128)}, u32[]{:S(2)}) copy-start(f32[256,256]{1,0:T(8,128)} %prior_ref.1) | copy-start | bytes 786436
  16.2 0.7 copy-start.4
  109.9 2.4 %collective-permute-start = (f32[528,256]{1,0:T(8,128)S(1)}, f32[528,256]{1,0:T(8,128)S(1)}, u32[]{:S(2)}, u32[]{:S(2)}) collective-permute-start(f32[528,256]{1,0:T(8,128)S(1)} %get-tuple-element.10.state_ref), channel_id=1, source_target_pairs={{0,1},{1,0},{2,3},{3,2},{4,5},{5,4},{6,7},{7,6},{8,9},{9,8},{10,11... | collective-permute-start | bytes 1622024 | tf_op jit(solution)/shard_map/ppermute | solution.py:530
  110.4 2.0 %collective-permute-start.1 = (f32[272,256]{1,0:T(8,128)S(1)}, f32[272,256]{1,0:T(8,128)S(1)}, u32[]{:S(2)}, u32[]{:S(2)}) collective-permute-start(f32[272,256]{1,0:T(8,128)S(1)} %get-tuple-element.11.info_ref), channel_id=1, source_target_pairs={{0,1},{1,0},{2,3},{3,2},{4,5},{5,4},{6,7},{7,6},{8,9},{9,8},{10,11... | collective-permute-start | bytes 835592 | tf_op jit(solution)/shard_map/ppermute | solution.py:531
  136.4 8.8 %collective-permute-start.2 = (f32[136,256]{1,0:T(8,128)S(1)}, f32[136,256]{1,0:T(8,128)S(1)}, u32[]{:S(2)}, u32[]{:S(2)}) collective-permute-start(f32[136,256]{1,0:T(8,128)S(1)} %shard_map.88), channel_id=1, source_target_pairs={{0,0},{1,16},{2,2},{3,18},{4,4},{5,20},{6,6},{7,22},{8,8},{9,24},{... | collective-permute-start | bytes 417800 | tf_op jit(solution)/shard_map/ppermute | solution.py:551
